TPU v7x, 32 devices: a whole 2x2x4 slice. The times are simulated.
32 devices in a mesh: dap: 16 (over z, y, core), dp: 2 (over x).
Axes of the slice: x: 2, y: 2, z: 4, core: 2. Of those that a mesh axis runs over, the one named last changes fastest.
Arguments:
- alignment_embedding: bfloat16 [32, 16, 256], P('dp', 'dap'), parts along dimension 0, may hold values from -6 to 6
- alignment_existing_flags: int32 [32, 16], P('dp', 'dap'), parts along dimension 0, may hold values 0 or 1
- couple_embedding: bfloat16 [32, 16, 128], P(('dp', 'dap')), parts along dimension 0, may hold values from -6 to 6
- alignment_scaling_factor: float32 [256], replicated, may hold values from 0.1 to 1.9
- couple_scaling_factor: float32 [128], replicated, may hold values from 0.1 to 1.9
- request_matrix: bfloat16 [256, 256], replicated, may hold values from -0.375 to 0.375
- lookup_matrix: bfloat16 [256, 256], replicated, may hold values from -0.375 to 0.375
- content_matrix: bfloat16 [256, 256], replicated, may hold values from -0.375 to 0.375
- switch_matrix: bfloat16 [256, 256], replicated, may hold values from -0.375 to 0.375
- final_projection_matrix: bfloat16 [256, 256], replicated, may hold values from -0.375 to 0.375
- couple_to_headterm_matrix: bfloat16 [128, 8], replicated, may hold values from -30 to 30
- increment_adjoint: bfloat16 [32, 16, 256], P('dp', 'dap'), parts along dimension 0, may hold values from -48 to 48
Outputs:
- alignment_increment: bfloat16 [32, 16, 256], P('dp', 'dap'), parts along dimension 0
- alignment_adjoint: bfloat16 [32, 16, 256], P('dp', 'dap'), parts along dimension 0
- couple_adjoint: bfloat16 [32, 16, 128], P(('dp', 'dap')), parts along dimension 0
- d_w_query: float32 [512, 256], P('dp'), parts along dimension 0
- d_w_key: float32 [512, 256], P('dp'), parts along dimension 0
- d_w_value: float32 [512, 256], P('dp'), parts along dimension 0
- d_w_gate: float32 [512, 256], P('dp'), parts along dimension 0
- d_w_out: float32 [512, 256], P('dp'), parts along dimension 0
- couple_headterm_adjoint: float32 [256, 8], P('dp'), parts along dimension 0
- d_msa_gain: float32 [512], P('dp'), parts along dimension 0
- couple_scaling_adjoint: float32 [256], P('dp'), parts along dimension 0
There are 2 independent parts, one for each index of `dp`. A program takes and returns all parts, laid end to end along the dimension named above; an argument that names none is the same for every part. Nothing has to cross between parts.
All inputs are finite; a program needn't handle non-finite values. No bound on the sum of `alignment_existing_flags` on one device may be relied on, other than what follows from the above.
Results may differ from a plain program's by a relative error of at most 0.012.
The roundings to bfloat16 on the way count: a program that leaves them out, or rounds other values in their place, can miss the bound.
Values may be sent and summed in bfloat16 or wider, within the bound.
A program may use at most 64 MiB of HBM per device.

v0:
```python
import jax
import jax.numpy as jnp
from jax import lax
from jax.sharding import PartitionSpec as P

ALIGN_FEATURES = 256
HEAD_NUMBER = 8
HEAD_DIMENSION = 32


EPS = 1e-05


def standardise_features(value, gain):
    mean = jnp.mean(value, axis=-1, keepdims=True)
    centered = value - mean
    variance = jnp.mean(centered * centered, axis=-1, keepdims=True)
    reciprocal_spread = lax.rsqrt(variance + EPS)
    standardised_lines = centered * reciprocal_spread
    return (standardised_lines, reciprocal_spread, standardised_lines * gain)


def standardise_features_adjoint(upstream_gradient, standardised_lines, reciprocal_spread, gain):
    rescaled_request = upstream_gradient * gain
    return reciprocal_spread * (
        rescaled_request
        - jnp.mean(rescaled_request, axis=-1, keepdims=True)
        - standardised_lines
        * jnp.mean(rescaled_request * standardised_lines, axis=-1, keepdims=True)
    )


def tensor_product(left, right):
    return lax.dot_general(
        left, right, (((0,), (0,)), ((), ())), preferred_element_type=jnp.float32
    )


def onward_one_line(
    alignment_line_content,
    line_filter_flags,
    couple_headwise_terms,
    alignment_scaling_factor,
    request_matrix,
    lookup_matrix,
    content_matrix,
    switch_matrix,
    final_projection_matrix,
):
    element_number = alignment_line_content.shape[0]
    standardised_lines, reciprocal_spread, rescaled_request = standardise_features(
        alignment_line_content.astype(jnp.float32), alignment_scaling_factor
    )
    input_arrays = rescaled_request.astype(jnp.bfloat16)
    query = (
        jnp.dot(input_arrays, request_matrix, preferred_element_type=jnp.float32)
        * HEAD_DIMENSION ** (-0.5)
    ).astype(jnp.bfloat16)
    keys = jnp.dot(input_arrays, lookup_matrix, preferred_element_type=jnp.float32).astype(
        jnp.bfloat16
    )
    values = jnp.dot(input_arrays, content_matrix, preferred_element_type=jnp.float32).astype(
        jnp.bfloat16
    )
    gate_sigmoid = jax.nn.sigmoid(
        jnp.dot(input_arrays, switch_matrix, preferred_element_type=jnp.float32)
    )
    query = query.reshape(element_number, HEAD_NUMBER, HEAD_DIMENSION)
    keys = keys.reshape(element_number, HEAD_NUMBER, HEAD_DIMENSION)
    values = values.reshape(element_number, HEAD_NUMBER, HEAD_DIMENSION)
    scores = jnp.einsum("ihd,jhd->ihj", query, keys, preferred_element_type=jnp.float32)
    scores = (
        scores
        + couple_headwise_terms.astype(jnp.float32)
        + (1000000000.0 * (line_filter_flags.astype(jnp.float32) - 1.0))[None, None, :]
    )
    probs = jax.nn.softmax(scores, axis=-1)
    probs_low = probs.astype(jnp.bfloat16)
    attention_probs = jnp.einsum(
        "ihj,jhd->ihd", probs_low, values, preferred_element_type=jnp.float32
    ).reshape(element_number, HEAD_NUMBER * HEAD_DIMENSION)
    weighted_values = (gate_sigmoid * attention_probs).astype(jnp.bfloat16)
    alignment_increment = jnp.dot(
        weighted_values, final_projection_matrix, preferred_element_type=jnp.float32
    ).astype(jnp.bfloat16)
    kept_intermediates = (
        standardised_lines,
        reciprocal_spread,
        input_arrays,
        query,
        keys,
        values,
        gate_sigmoid,
        attention_probs,
        weighted_values,
        probs,
    )
    return (alignment_increment, kept_intermediates)


def reverse_one_line(
    line_adjoint_routine,
    kept_intermediates,
    alignment_scaling_factor,
    request_matrix,
    lookup_matrix,
    content_matrix,
    switch_matrix,
    final_projection_matrix,
):
    (
        standardised_lines,
        reciprocal_spread,
        input_arrays,
        query,
        keys,
        values,
        gate_sigmoid,
        attention_probs,
        weighted_values,
        probs,
    ) = kept_intermediates
    element_number = line_adjoint_routine.shape[0]
    probs_low = probs.astype(jnp.bfloat16)
    upstream_gradient = lax.dot_general(
        line_adjoint_routine,
        final_projection_matrix,
        (((1,), (1,)), ((), ())),
        preferred_element_type=jnp.float32,
    )
    d_attn = (upstream_gradient * gate_sigmoid).astype(jnp.bfloat16)
    gate_logit_gradient = (
        upstream_gradient * attention_probs * gate_sigmoid * (1.0 - gate_sigmoid)
    ).astype(jnp.bfloat16)
    d_attn_heads = d_attn.reshape(element_number, HEAD_NUMBER, HEAD_DIMENSION)
    d_probs = jnp.einsum("ihd,jhd->ihj", d_attn_heads, values, preferred_element_type=jnp.float32)
    affinity_adjoint = probs * (d_probs - jnp.sum(probs * d_probs, axis=-1, keepdims=True))
    d_low = affinity_adjoint.astype(jnp.bfloat16)
    query_gradient = (
        (
            jnp.einsum("ihj,jhd->ihd", d_low, keys, preferred_element_type=jnp.float32)
            * HEAD_DIMENSION ** (-0.5)
        )
        .astype(jnp.bfloat16)
        .reshape(element_number, HEAD_NUMBER * HEAD_DIMENSION)
    )
    key_gradient = (
        jnp.einsum("ihj,ihd->jhd", d_low, query, preferred_element_type=jnp.float32)
        .astype(jnp.bfloat16)
        .reshape(element_number, HEAD_NUMBER * HEAD_DIMENSION)
    )
    value_gradient = (
        jnp.einsum("ihj,ihd->jhd", probs_low, d_attn_heads, preferred_element_type=jnp.float32)
        .astype(jnp.bfloat16)
        .reshape(element_number, HEAD_NUMBER * HEAD_DIMENSION)
    )
    backward_result = (((1,), (1,)), ((), ()))
    argument_adjoints = lax.dot_general(
        query_gradient, request_matrix, backward_result, preferred_element_type=jnp.float32
    )
    argument_adjoints = argument_adjoints + lax.dot_general(
        key_gradient, lookup_matrix, backward_result, preferred_element_type=jnp.float32
    )
    argument_adjoints = argument_adjoints + lax.dot_general(
        value_gradient, content_matrix, backward_result, preferred_element_type=jnp.float32
    )
    argument_adjoints = argument_adjoints + lax.dot_general(
        gate_logit_gradient, switch_matrix, backward_result, preferred_element_type=jnp.float32
    )
    line_adjoint = standardise_features_adjoint(
        argument_adjoints, standardised_lines, reciprocal_spread, alignment_scaling_factor
    ).astype(jnp.bfloat16)
    matrix_adjoints = (
        tensor_product(input_arrays, query_gradient),
        tensor_product(input_arrays, key_gradient),
        tensor_product(input_arrays, value_gradient),
        tensor_product(input_arrays, gate_logit_gradient),
        tensor_product(weighted_values, line_adjoint_routine),
        jnp.sum(argument_adjoints * standardised_lines, axis=0),
    )
    return (line_adjoint, affinity_adjoint, matrix_adjoints)


def on_device(
    alignment_embedding,
    alignment_existing_flags,
    couple_embedding,
    alignment_scaling_factor,
    couple_scaling_factor,
    request_matrix,
    lookup_matrix,
    content_matrix,
    switch_matrix,
    final_projection_matrix,
    couple_to_headterm_matrix,
    increment_adjoint,
):
    filter_shared = alignment_existing_flags.astype(jnp.bfloat16)
    alignment_line_embedding, alignment_line_flags = (
        lax.all_to_all(alignment_embedding, "dap", split_axis=0, concat_axis=1, tiled=True),
        lax.all_to_all(filter_shared, "dap", split_axis=0, concat_axis=1, tiled=True),
    )
    pair_hat, pair_inv, pair_scaled = standardise_features(
        couple_embedding.astype(jnp.float32), couple_scaling_factor
    )
    pair_ln = pair_scaled.astype(jnp.bfloat16)
    bias_rows = jnp.einsum(
        "ijc,ch->ihj", pair_ln, couple_to_headterm_matrix, preferred_element_type=jnp.float32
    ).astype(jnp.bfloat16)
    couple_headwise_terms = lax.all_gather(bias_rows, "dap", axis=0, tiled=True)

    def onward_loop_step(carry, loop_elements):
        alignment_increment, kept_intermediates = onward_one_line(
            loop_elements[0],
            loop_elements[1],
            couple_headwise_terms,
            alignment_scaling_factor,
            request_matrix,
            lookup_matrix,
            content_matrix,
            switch_matrix,
            final_projection_matrix,
        )
        return (carry, (alignment_increment, kept_intermediates))

    unused_value, (row_updates, all_saved_residuals) = lax.scan(
        onward_loop_step, None, (alignment_line_embedding, alignment_line_flags)
    )
    update_out = lax.all_to_all(row_updates, "dap", split_axis=1, concat_axis=0, tiled=True)
    seq_grad = lax.all_to_all(increment_adjoint, "dap", split_axis=0, concat_axis=1, tiled=True)
    amino_positions = alignment_line_embedding.shape[1]
    span_length = HEAD_NUMBER * HEAD_DIMENSION
    blank_matrix = (
        jnp.zeros((ALIGN_FEATURES, span_length), jnp.float32),
        jnp.zeros((ALIGN_FEATURES, span_length), jnp.float32),
        jnp.zeros((ALIGN_FEATURES, span_length), jnp.float32),
        jnp.zeros((ALIGN_FEATURES, span_length), jnp.float32),
        jnp.zeros((span_length, ALIGN_FEATURES), jnp.float32),
        jnp.zeros((ALIGN_FEATURES,), jnp.float32),
    )

    def backward_step(carry, loop_elements):
        bias_sum, subtotal_list = carry
        line_adjoint, affinity_adjoint, matrix_adjoints = reverse_one_line(
            loop_elements[0],
            loop_elements[1],
            alignment_scaling_factor,
            request_matrix,
            lookup_matrix,
            content_matrix,
            switch_matrix,
            final_projection_matrix,
        )
        subtotal_list = tuple((a + b for a, b in zip(subtotal_list, matrix_adjoints)))
        return ((bias_sum + affinity_adjoint, subtotal_list), line_adjoint)

    beginning_shift = (
        jnp.zeros((amino_positions, HEAD_NUMBER, amino_positions), jnp.float32),
        blank_matrix,
    )
    (bias_term, subtotal_list), line_adjoint_list = lax.scan(
        backward_step, beginning_shift, (seq_grad, all_saved_residuals)
    )
    additive_term_adjoint = lax.psum_scatter(bias_term, "dap", scatter_dimension=0, tiled=True)
    d_pln = jnp.einsum(
        "ihj,ch->ijc",
        additive_term_adjoint,
        couple_to_headterm_matrix.astype(jnp.float32),
        precision=lax.Precision.HIGHEST,
    )
    w_bias_part = jnp.einsum(
        "ijc,ihj->ch",
        pair_ln.astype(jnp.float32),
        additive_term_adjoint,
        precision=lax.Precision.HIGHEST,
    )
    pair_gain_part = jnp.sum(d_pln * pair_hat, axis=(0, 1))
    couple_adjoint = standardise_features_adjoint(
        d_pln, pair_hat, pair_inv, couple_scaling_factor
    ).astype(jnp.bfloat16)
    totals = lax.psum(
        (
            subtotal_list[0],
            subtotal_list[1],
            subtotal_list[2],
            subtotal_list[3],
            subtotal_list[4],
            w_bias_part,
            subtotal_list[5],
            pair_gain_part,
        ),
        "dap",
    )
    alignment_adjoint = lax.all_to_all(
        line_adjoint_list, "dap", split_axis=1, concat_axis=0, tiled=True
    )
    return (
        update_out,
        alignment_adjoint,
        couple_adjoint,
        totals[0],
        totals[1],
        totals[2],
        totals[3],
        totals[4],
        totals[5],
        totals[6],
        totals[7],
    )


def solution(mesh):
    in_specs = (
        P("dp", "dap", None),
        P("dp", "dap"),
        P(("dp", "dap"), None, None),
        P(),
        P(),
        P(),
        P(),
        P(),
        P(),
        P(),
        P(),
        P("dp", "dap", None),
    )
    out_specs = (
        P("dp", "dap", None),
        P("dp", "dap", None),
        P(("dp", "dap"), None, None),
        P("dp", None),
        P("dp", None),
        P("dp", None),
        P("dp", None),
        P("dp", None),
        P("dp", None),
        P("dp"),
        P("dp"),
    )
    return jax.shard_map(
        on_device, mesh=mesh, in_specs=in_specs, out_specs=out_specs, check_vma=False
    )
```

profile of v0, /device:TPU:0, one launch (start us, length us, event | category | flops | bytes accessed | tf_op | source)
XLA Modules:
  0.0 243.5 jit_solution(16372690872006035261)
XLA Ops:
  7.2 0.7 convert_bitcast_fusion.2
  7.9 0.7 copy.76
  8.6 7.4 %all-to-all-start.1 = ((bf16[16,1,1]{2,1,0:T(2,128)(2,1)}), bf16[16,1,1]{2,1,0:T(2,128)(2,1)S(1)}, u32[]{:S(2)}, u32[]{:S(2)}) async-start(bf16[16,1,1]{2,1,0:T(2,128)(2,1)} %copy.76), calls=%async_computation.1 | async-start | bytes 16384 | tf_op jit(solution)/shard_map/all_to_all | solution.py:201
  16.0 0.7 copy-done.9
  17.0 0.5 broadcast.222
  17.5 0.7 reduce.9
  18.2 0.6 reshape.335
  18.9 0.6 reduce.8
  19.6 0.6 reshape.339
  20.4 21.8 %all-gather = bf16[128,16]{1,0:T(8,128)(2,1)S(1)} all-gather(bf16[8,16]{1,0:T(8,128)(2,1)S(1)} %fusion.14), channel_id=2, replica_groups=mesh['dap'=16,'dp'=2] {'dap'}, dimensions={0}, use_global_device_ids=true | all-gather | bytes 4352 | tf_op jit(solution)/shard_map/all_gather | solution.py:210
  42.3 0.7 copy-done.15
  43.0 0.6 dynamic-slice.6
  43.5 3.5 %all-to-all-start = ((bf16[16,2,128]{2,1,0:T(2,128)(2,1)}), bf16[16,2,128]{2,1,0:T(2,128)(2,1)S(1)}, u32[]{:S(2)}, u32[]{:S(2)}) async-start(bf16[16,2,128]{2,1,0:T(2,128)(2,1)} %reshape.335), calls=%async_computation | async-start | bytes 16384 | tf_op jit(solution)/shard_map/all_to_all | solution.py:200
  47.2 6.1 %all-to-all-done = bf16[16,2,128]{2,1,0:T(2,128)(2,1)S(1)} async-done(((bf16[16,2,128]{2,1,0:T(2,128)(2,1)}), bf16[16,2,128]{2,1,0:T(2,128)(2,1)S(1)}, u32[]{:S(2)}, u32[]{:S(2)}) %all-to-all-start) | async-done | bytes 8224 | tf_op jit(solution)/shard_map/all_to_all | solution.py:200
  53.3 3.6 %all-to-all-start.3 = ((bf16[16,2,128]{2,1,0:T(2,128)(2,1)}), bf16[16,2,128]{2,1,0:T(2,128)(2,1)S(1)}, u32[]{:S(2)}, u32[]{:S(2)}) async-start(bf16[16,2,128]{2,1,0:T(2,128)(2,1)} %reshape.339), calls=%async_computation.3 | async-start | bytes 16384 | tf_op jit(solution)/shard_map/all_to_all | solution.py:230
  57.5 0.4 copy-done.6
  58.0 0.7 copy-done.8
  59.4 0.3 fusion.85
  59.9 3.3 %all-to-all-done.3 = bf16[16,2,128]{2,1,0:T(2,128)(2,1)S(1)} async-done(((bf16[16,2,128]{2,1,0:T(2,128)(2,1)}), bf16[16,2,128]{2,1,0:T(2,128)(2,1)S(1)}, u32[]{:S(2)}, u32[]{:S(2)}) %all-to-all-start.3) | async-done | bytes 8224 | tf_op jit(solution)/shard_map/all_to_all | solution.py:230
  63.4 0.2 multiply_convert_fusion
  64.6 0.9 fusion.60
  65.8 1.0 fusion.77
  66.9 0.7 reduce.10
  67.6 0.6 reshape.337
  68.2 3.5 %all-to-all-start.2 = ((bf16[16,2,128]{2,1,0:T(2,128)(2,1)}), bf16[16,2,128]{2,1,0:T(2,128)(2,1)S(1)}, u32[]{:S(2)}, u32[]{:S(2)}) async-start(bf16[16,2,128]{2,1,0:T(2,128)(2,1)} %reshape.337), calls=%async_computation.2 | async-start | bytes 16384 | tf_op jit(solution)/shard_map/all_to_all | solution.py:229
  71.9 61.9 %all-reduce = f32[16,8,16]{2,1,0:T(8,128)S(1)} all-reduce(f32[16,8,16]{2,1,0:T(8,128)S(1)} %copy.92), channel_id=3, replica_groups=mesh['dap'=16,'dp'=2] {'dap'}, use_global_device_ids=true, to_apply=%region_9.10.clone | all-reduce | flops 2048 | bytes 16384
  133.9 1.0 fusion.56
  134.9 1.0 fusion.75
  136.1 1.0 fusion.73
  137.3 1.0 fusion.79
  138.3 0.3 fusion.35
  138.7 0.7 fusion.55
  139.4 0.7 reduce.11
  140.1 0.6 reshape.341
  140.7 3.5 %all-to-all-start.4 = ((bf16[16,2,128]{2,1,0:T(2,128)(2,1)}), bf16[16,2,128]{2,1,0:T(2,128)(2,1)S(1)}, u32[]{:S(2)}, u32[]{:S(2)}) async-start(bf16[16,2,128]{2,1,0:T(2,128)(2,1)} %reshape.341), calls=%async_computation.4 | async-start | bytes 16384 | tf_op jit(solution)/shard_map/all_to_all | solution.py:294
  144.2 0.8 fusion.65
  145.0 35.1 %all-reduce.1 = (f32[128,8]{0,1:T(8,128)}, f32[256]{0:T(256)}, f32[128]{0:T(128)}) all-reduce(f32[128,8]{0,1:T(8,128)S(1)} %fusion.65, f32[256]{0:T(256)S(1)} %get-tuple-element.100, f32[128]{0:T(128)S(1)} %get-tuple-element.103), channel_id=1, replica_groups=mesh['dap'=16,'dp'=2] {'dap'}, use_global_device_ids=true, to_apply=%region_17.18 | all-reduce | flops 1408 | bytes 11264 | tf_op jit(solution)/shard_map/psum | solution.py:281
  180.2 0.6 copy.132
  180.8 0.6 copy.131
  181.4 49.7 %all-reduce.5.cloned.1.call-done = (f32[256,256]{1,0:T(8,128)}, f32[256,256]{1,0:T(8,128)}, f32[256,256]{1,0:T(8,128)}, f32[256,256]{1,0:T(8,128)}, f32[256,256]{1,0:T(8,128)}) async-done(((f32[256,256]{1,0:T(8,128)}, f32[256,256]{1,0:T(8,128)}, f32[256,256]{1,0:T(8,128)}, f32[256,256]{1,0:T(8,128)}, f32[256,256]{1,0:T(8,128)}), (f32[256,256]{1,0:T(8,128)}, f32[256,256]{1,0:T(8,128)}, f32[256,256]{1,0:T(8,128)}, ...) | async-done | bytes 1310736 | tf_op jit(solution)/shard_map/psum | solution.py:281
  231.1 1.7 copy.142
  232.8 0.7 copy.143
  233.5 0.3 copy-done.4
  233.9 0.7 copy.144
  234.6 0.3 copy-done.3
  234.9 0.7 copy.145
  235.6 0.3 copy-done.2
  236.0 0.7 copy.146
  (80 shorter events, 4.8 us)
Async XLA Ops:
  7.2 56.2 %copy-start = (bf16[256,256]{1,0:T(8,128)(2,1)S(1)}, bf16[256,256]{1,0:T(8,128)(2,1)}, u32[]{:S(2)}) copy-start(bf16[256,256]{1,0:T(8,128)(2,1)} %param.20) | copy-start | bytes 393220
  8.6 35.0 %all-to-all-start.1 = ((bf16[16,1,1]{2,1,0:T(2,128)(2,1)}), bf16[16,1,1]{2,1,0:T(2,128)(2,1)S(1)}, u32[]{:S(2)}, u32[]{:S(2)}) async-start(bf16[16,1,1]{2,1,0:T(2,128)(2,1)} %copy.76), calls=%async_computation.1 | async-start | bytes 16384 | tf_op jit(solution)/shard_map/all_to_all | solution.py:201
  16.0 0.7 copy-start.9
  16.7 0.8 copy-start.11
  18.2 0.7 copy-start.12
  19.5 0.7 copy-start.13
  19.5 0.7 copy-start.14
  42.2 15.1 %copy-start.7 = (bf16[256,256]{1,0:T(8,128)(2,1)S(1)}, bf16[256,256]{1,0:T(8,128)(2,1)}, u32[]{:S(2)}) copy-start(bf16[256,256]{1,0:T(8,128)(2,1)} %param.18) | copy-start | bytes 393220
  42.3 0.7 copy-start.15
  43.5 9.8 %all-to-all-start = ((bf16[16,2,128]{2,1,0:T(2,128)(2,1)}), bf16[16,2,128]{2,1,0:T(2,128)(2,1)S(1)}, u32[]{:S(2)}, u32[]{:S(2)}) async-start(bf16[16,2,128]{2,1,0:T(2,128)(2,1)} %reshape.335), calls=%async_computation | async-start | bytes 16384 | tf_op jit(solution)/shard_map/all_to_all | solution.py:200
  53.3 4.0 %copy-start.10 = (f32[256]{0:T(256)S(1)}, f32[256]{0:T(256)}, u32[]{:S(2)}) copy-start(f32[256]{0:T(256)} %param.15) | copy-start | bytes 3076
  53.3 9.9 %all-to-all-start.3 = ((bf16[16,2,128]{2,1,0:T(2,128)(2,1)}), bf16[16,2,128]{2,1,0:T(2,128)(2,1)S(1)}, u32[]{:S(2)}, u32[]{:S(2)}) async-start(bf16[16,2,128]{2,1,0:T(2,128)(2,1)} %reshape.339), calls=%async_computation.3 | async-start | bytes 16384 | tf_op jit(solution)/shard_map/all_to_all | solution.py:230
  56.9 0.9 copy-start.6
  57.8 0.9 copy-start.8
  59.8 3.4 %copy-start.1 = (bf16[256,256]{1,0:T(8,128)(2,1)S(1)}, bf16[256,256]{1,0:T(8,128)(2,1)}, u32[]{:S(2)}) copy-start(bf16[256,256]{1,0:T(8,128)(2,1)} %param.21) | copy-start | bytes 393220
  68.2 72.5 %all-to-all-start.2 = ((bf16[16,2,128]{2,1,0:T(2,128)(2,1)}), bf16[16,2,128]{2,1,0:T(2,128)(2,1)S(1)}, u32[]{:S(2)}, u32[]{:S(2)}) async-start(bf16[16,2,128]{2,1,0:T(2,128)(2,1)} %reshape.337), calls=%async_computation.2 | async-start | bytes 16384 | tf_op jit(solution)/shard_map/all_to_all | solution.py:229
  71.7 159.4 %all-reduce.5.cloned.1.call-start = ((), (), s32[]{:S(2)}) async-start(), calls=%async_computation.5 | async-start | bytes 2621440 | tf_op jit(solution)/shard_map/psum | solution.py:281
  140.7 40.1 %all-to-all-start.4 = ((bf16[16,2,128]{2,1,0:T(2,128)(2,1)}), bf16[16,2,128]{2,1,0:T(2,128)(2,1)S(1)}, u32[]{:S(2)}, u32[]{:S(2)}) async-start(bf16[16,2,128]{2,1,0:T(2,128)(2,1)} %reshape.341), calls=%async_computation.4 | async-start | bytes 16384 | tf_op jit(solution)/shard_map/all_to_all | solution.py:294
  231.1 1.7 copy-start.5
  232.8 1.0 copy-start.4
  233.9 1.0 copy-start.3
  234.9 1.0 copy-start.2
Sparse Core Ops, SparseCore 0:
  138.8 92.2 all-reduce.4
where the time goes:
time: 244 us
  blocking collectives  119 us (49%)
  waiting for transfers between devices  59.1 us (24%)
  starting transfers between devices  21.4 us (9%)
  local copies, waits for them, and re-layouts  14.6 us (6%)
  between operations  14.3 us (6%)
  matrix products  9.75 us (4%)
  other arithmetic  5.37 us (2%)
    unnamed x1, blocking collectives  61.9 us
    psum x1, waiting for transfers between devices, on_device(): lax.psum((subtotal_list[0], subtotal_list[1], subtotal_list[2], subtotal_...  49.7 us
    psum x1, blocking collectives, on_device(): lax.psum((subtotal_list[0], subtotal_list[1], subtotal_list[2], subtotal_...  35.1 us
    all_gather x1, blocking collectives, on_device(): couple_headwise_terms = lax.all_gather(bias_rows, 'dap', axis=0, tiled=True)  21.8 us
    unnamed x49, local copies, waits for them, and re-layouts  12.9 us
    all_to_all x1, starting transfers between devices, on_device(): lax.all_to_all(filter_shared, 'dap', split_axis=0, concat_axis=1, tiled=T...  7.39 us
    all_to_all x1, waiting for transfers between devices, on_device(): lax.all_to_all(alignment_embedding, 'dap', split_axis=0, concat_axis=1, t...  6.09 us
    dot_general x5, matrix products, tensor_product(): lax.dot_general(left, right, (((0,), (0,)), ((), ())), preferred_element_...  4.99 us
  transfers between devices with their start and end apart: 6, of which 3 were waited for; matrix products, arithmetic and copies ran while one was open for 6% of the time, Pallas kernels for 0%

commit v1 on v0

--- a/solution.py
+++ b/solution.py
@@ -1,6 +1,8 @@
 import jax
 import jax.numpy as jnp
 from jax import lax
+from jax.experimental import pallas as pl
+from jax.experimental.pallas import tpu as pltpu
 from jax.sharding import PartitionSpec as P
 
 ALIGN_FEATURES = 256
@@ -181,6 +183,385 @@
     return (line_adjoint, affinity_adjoint, matrix_adjoints)
 
 
+LANES = 128
+ROW_TILE = 16
+
+
+def whole_part_fits(alignment_embedding, couple_embedding):
+    sequences, owned, _ = alignment_embedding.shape
+    owned_pairs, residues, pair_channels = couple_embedding.shape
+    devices = lax.axis_size("dap")
+    return (
+        owned == 1
+        and owned_pairs == 1
+        and devices == residues
+        and devices % 4 == 0
+        and HEAD_NUMBER * residues == LANES
+        and pair_channels == LANES
+        and sequences == residues
+        and sequences % ROW_TILE == 0
+    )
+
+
+def gather_kernel(devices, msa_ref, flag_ref, pair_ref, grad_ref, all_ref, send_sem, recv_sem):
+    me = lax.axis_index("dap")
+    rows = msa_ref.shape[0]
+    lanes = pair_ref.shape[1]
+    planes = devices // 4
+    core = lax.rem(me, 2)
+    row = lax.rem(me // 2, 2)
+    sibling = me + 1 - 2 * core
+    across = me + 2 - 4 * row
+    far = [lax.rem(me + 4 * k, devices) for k in range(1, planes)]
+    far_across = [lax.rem(across + 4 * k, devices) for k in range(1, planes)]
+
+    barrier = pltpu.get_barrier_semaphore()
+    for peer in far + [across, sibling]:
+        pl.semaphore_signal(
+            barrier, inc=1, device_id={"dap": peer}, device_id_type=pl.DeviceIdType.MESH
+        )
+    all_ref[me, 0:rows, :] = msa_ref[...]
+    all_ref[me, rows : 2 * rows, :] = grad_ref[...]
+    all_ref[me, 2 * rows :, 0:lanes] = pair_ref[...]
+    all_ref[me, 2 * rows :, lanes:] = jnp.broadcast_to(
+        flag_ref[...].astype(jnp.float32), (rows, lanes)
+    ).astype(jnp.bfloat16)
+    pl.semaphore_wait(barrier, planes + 1)
+
+    sent = []
+
+    def send(slot, peer):
+        copy = pltpu.make_async_remote_copy(
+            src_ref=all_ref.at[slot],
+            dst_ref=all_ref.at[slot],
+            send_sem=send_sem.at[len(sent)],
+            recv_sem=recv_sem.at[slot],
+            device_id={"dap": peer},
+            device_id_type=pl.DeviceIdType.MESH,
+        )
+        copy.start()
+        sent.append(copy)
+
+    def arrive(slot):
+        pltpu.make_async_remote_copy(
+            src_ref=all_ref.at[slot],
+            dst_ref=all_ref.at[slot],
+            send_sem=send_sem.at[0],
+            recv_sem=recv_sem.at[slot],
+            device_id={"dap": sibling},
+            device_id_type=pl.DeviceIdType.MESH,
+        ).wait_recv()
+
+    for peer in far:
+        send(me, peer)
+    send(me, across)
+    send(me, sibling)
+    arrive(across)
+    send(across, sibling)
+    for slot in far:
+        arrive(slot)
+        send(slot, across)
+        send(slot, sibling)
+    for slot in far_across:
+        arrive(slot)
+        send(slot, sibling)
+    sibling_across = sibling + 2 - 4 * row
+    for k in range(planes):
+        arrive(lax.rem(sibling + 4 * k, devices))
+        arrive(lax.rem(sibling_across + 4 * k, devices))
+    for copy in sent:
+        copy.wait_send()
+
+
+def iota(shape, dimension):
+    return lax.broadcasted_iota(jnp.int32, shape, dimension)
+
+
+def one_where(condition):
+    return jnp.where(condition, 1.0, 0.0).astype(jnp.bfloat16)
+
+
+def product(left, right, contract=((1,), (0,))):
+    return lax.dot_general(left, right, (contract, ((), ())), preferred_element_type=jnp.float32)
+
+
+OUTER = ((1,), (1,))
+INNER = ((0,), (0,))
+
+
+def split_product(left, right, contract=((1,), (0,)), split_left=True):
+    wide = left if split_left else right
+    upper = wide.astype(jnp.bfloat16)
+    lower = (wide - upper.astype(jnp.float32)).astype(jnp.bfloat16)
+    if split_left:
+        return product(upper, right, contract) + product(lower, right, contract)
+    return product(left, upper, contract) + product(left, lower, contract)
+
+
+def over_group(value, width, combine):
+    lane = iota(value.shape, 1)
+    size = value.shape[1]
+    step = 1
+    while step < width:
+        other = jnp.where(
+            (lane // step) % 2 == 0,
+            pltpu.roll(value, size - step, 1),
+            pltpu.roll(value, step, 1),
+        )
+        value = combine(value, other)
+        step *= 2
+    return value
+
+
+def part_kernel(
+    all_ref,
+    gain_ref,
+    pair_gain_ref,
+    request_ref,
+    lookup_ref,
+    content_ref,
+    switch_ref,
+    final_ref,
+    headterm_ref,
+    update_ref,
+    adjoint_ref,
+    pair_adjoint_ref,
+    d_query_ref,
+    d_key_ref,
+    d_value_ref,
+    d_gate_ref,
+    d_out_ref,
+    d_headterm_ref,
+    d_gain_ref,
+    d_pair_gain_ref,
+    pair_rows_ref,
+):
+    me = lax.axis_index("dap")
+    residues = all_ref.shape[0]
+    sequences = all_ref.shape[1] // 3
+    channels = all_ref.shape[2]
+    tokens = residues * sequences
+    span = HEAD_NUMBER * HEAD_DIMENSION
+    columns = HEAD_NUMBER * residues
+    gain = gain_ref[...]
+    pair_gain = pair_gain_ref[...]
+
+    pair_lanes = pair_gain.shape[1]
+    pair_raw = all_ref[:, 2 * sequences :, 0:pair_lanes].reshape(residues * residues, pair_lanes)
+    pair_hat, pair_inv, pair_scaled = standardise_features(
+        pair_raw.astype(jnp.float32), pair_gain
+    )
+    pair_ln = pair_scaled.astype(jnp.bfloat16)
+    spread = one_where(
+        iota((HEAD_NUMBER, columns), 0) == iota((HEAD_NUMBER, columns), 1) // residues
+    )
+    headterm_wide = product(headterm_ref[...], spread).astype(jnp.bfloat16)
+    pair_shape = (residues * residues, columns)
+    same_key = iota(pair_shape, 0) % residues == iota(pair_shape, 1) % residues
+    bias = jnp.sum(
+        jnp.where(same_key, product(pair_ln, headterm_wide), 0.0).reshape(
+            residues, residues, columns
+        ),
+        axis=1,
+    )
+    bias = bias.astype(jnp.bfloat16).astype(jnp.float32)
+
+    flag_lane = iota((sequences, columns), 1) % residues
+    flags = jnp.zeros((sequences, columns), jnp.float32)
+    for j in range(residues):
+        flags = jnp.where(
+            flag_lane == j, all_ref[j, 2 * sequences :, pair_lanes:].astype(jnp.float32), flags
+        )
+    fill = 1000000000.0 * (flags - 1.0)
+
+    square = (tokens, tokens)
+    reorder = one_where(
+        (iota(square, 0) // residues == iota(square, 1) % sequences)
+        & (iota(square, 0) % residues == iota(square, 1) // sequences)
+    )
+    raw = product(reorder, all_ref[:, 0:sequences, :].reshape(tokens, channels))
+    grad = product(
+        reorder, all_ref[:, sequences : 2 * sequences, :].reshape(tokens, channels)
+    ).astype(jnp.bfloat16)
+
+    hat, inv, scaled = standardise_features(raw, gain)
+    x = scaled.astype(jnp.bfloat16)
+    query = (product(x, request_ref[...]) * HEAD_DIMENSION ** (-0.5)).astype(jnp.bfloat16)
+    keys = product(x, lookup_ref[...]).astype(jnp.bfloat16)
+    values = product(x, content_ref[...]).astype(jnp.bfloat16)
+    gate = jax.nn.sigmoid(product(x, switch_ref[...]))
+    upstream = product(grad, final_ref[...], OUTER)
+    d_attn = (upstream * gate).astype(jnp.bfloat16)
+
+    head_shape = (columns, span)
+    own_head = iota(head_shape, 0) // residues == iota(head_shape, 1) // HEAD_DIMENSION
+    own_head_one = one_where(own_head)
+
+    def rows_of(value, s):
+        return value[s * residues : (s + 1) * residues]
+
+    def by_head(value):
+        return jnp.concatenate([value] * HEAD_NUMBER, axis=0) * own_head_one
+
+    def fold_heads(value):
+        return jnp.sum(
+            jnp.where(own_head, value, 0.0).reshape(HEAD_NUMBER, residues, span), axis=0
+        )
+
+    every = range(sequences)
+    wide_keys = [by_head(rows_of(keys, s)) for s in every]
+    wide_values = [by_head(rows_of(values, s)) for s in every]
+    scores = jnp.concatenate(
+        [
+            product(rows_of(query, s), wide_keys[s], OUTER) + bias + fill[s : s + 1]
+            for s in every
+        ],
+        axis=0,
+    )
+    scores = jnp.exp(scores - over_group(scores, residues, jnp.maximum))
+    probs = scores / over_group(scores, residues, jnp.add)
+    probs_low = probs.astype(jnp.bfloat16)
+    d_probs = jnp.concatenate(
+        [product(rows_of(d_attn, s), wide_values[s], OUTER) for s in every], axis=0
+    )
+    d_scores = probs * (d_probs - over_group(probs * d_probs, residues, jnp.add))
+    d_low = d_scores.astype(jnp.bfloat16)
+    attended = jnp.concatenate(
+        [product(rows_of(probs_low, s), wide_values[s]) for s in every], axis=0
+    )
+    weighted = (gate * attended).astype(jnp.bfloat16)
+    d_glog = (upstream * attended * gate * (1.0 - gate)).astype(jnp.bfloat16)
+    d_query = jnp.concatenate(
+        [product(rows_of(d_low, s), wide_keys[s]) for s in every], axis=0
+    )
+    d_query = (d_query * HEAD_DIMENSION ** (-0.5)).astype(jnp.bfloat16)
+    d_keys = jnp.concatenate(
+        [fold_heads(product(rows_of(d_low, s), rows_of(query, s), INNER)) for s in every], axis=0
+    ).astype(jnp.bfloat16)
+    d_values = jnp.concatenate(
+        [fold_heads(product(rows_of(probs_low, s), rows_of(d_attn, s), INNER)) for s in every],
+        axis=0,
+    ).astype(jnp.bfloat16)
+
+    d_query_ref[...] = product(x, d_query, INNER)
+    d_key_ref[...] = product(x, d_keys, INNER)
+    d_value_ref[...] = product(x, d_values, INNER)
+    d_gate_ref[...] = product(x, d_glog, INNER)
+    d_out_ref[...] = product(weighted, grad, INNER)
+
+    pick_shape = (sequences, tokens)
+    pick = one_where(iota(pick_shape, 1) == iota(pick_shape, 0) * residues + me)
+    update_ref[...] = product(
+        product(pick, weighted).astype(jnp.bfloat16), final_ref[...]
+    ).astype(jnp.bfloat16)
+
+    d_x = product(d_query, request_ref[...], OUTER)
+    d_x = d_x + product(d_keys, lookup_ref[...], OUTER)
+    d_x = d_x + product(d_values, content_ref[...], OUTER)
+    d_x = d_x + product(d_glog, switch_ref[...], OUTER)
+    d_gain_ref[...] = jnp.sum(d_x * hat, axis=0, keepdims=True)
+    d_msa = standardise_features_adjoint(d_x, hat, inv, gain).astype(jnp.bfloat16)
+    adjoint_ref[...] = product(pick, d_msa).astype(jnp.bfloat16)
+
+    d_bias = jnp.sum(d_scores.reshape(sequences, residues, columns), axis=0)
+    d_bias = jnp.where(
+        same_key,
+        jnp.broadcast_to(d_bias[:, None, :], (residues, residues, columns)).reshape(pair_shape),
+        0.0,
+    )
+    d_pln = split_product(d_bias, headterm_wide, OUTER)
+    d_headterm = split_product(pair_ln, d_bias, INNER, split_left=False)
+    d_headterm_ref[...] = jnp.sum(
+        d_headterm.T.reshape(HEAD_NUMBER, residues, pair_lanes), axis=1
+    )
+    d_pair_gain_ref[...] = jnp.sum(d_pln * pair_hat, axis=0, keepdims=True)
+    pair_rows_ref[...] = (
+        standardise_features_adjoint(d_pln, pair_hat, pair_inv, pair_gain)
+        .astype(jnp.bfloat16)
+        .reshape(residues, residues, pair_lanes)
+    )
+    pair_adjoint_ref[...] = pair_rows_ref[me]
+
+
+def on_device_whole_part(
+    alignment_embedding,
+    alignment_existing_flags,
+    couple_embedding,
+    alignment_scaling_factor,
+    couple_scaling_factor,
+    request_matrix,
+    lookup_matrix,
+    content_matrix,
+    switch_matrix,
+    final_projection_matrix,
+    couple_to_headterm_matrix,
+    increment_adjoint,
+):
+    sequences, _, channels = alignment_embedding.shape
+    _, residues, pair_channels = couple_embedding.shape
+    devices = lax.axis_size("dap")
+    vmem = pl.BlockSpec(memory_space=pltpu.VMEM)
+    gathered = pl.pallas_call(
+        lambda *refs: gather_kernel(devices, *refs),
+        out_shape=jax.ShapeDtypeStruct((devices, 3 * sequences, channels), jnp.bfloat16),
+        in_specs=[vmem] * 4,
+        out_specs=vmem,
+        scratch_shapes=[
+            pltpu.SemaphoreType.DMA((devices - 1,)),
+            pltpu.SemaphoreType.DMA((devices,)),
+        ],
+        compiler_params=pltpu.CompilerParams(collective_id=0, has_side_effects=True),
+        name="gather_part",
+    )(
+        alignment_embedding.reshape(sequences, channels),
+        alignment_existing_flags,
+        couple_embedding.reshape(residues, pair_channels),
+        increment_adjoint.reshape(sequences, channels),
+    )
+    span = HEAD_NUMBER * HEAD_DIMENSION
+    weight = jax.ShapeDtypeStruct((channels, span), jnp.float32)
+    outs = pl.pallas_call(
+        part_kernel,
+        out_shape=(
+            jax.ShapeDtypeStruct((sequences, channels), jnp.bfloat16),
+            jax.ShapeDtypeStruct((sequences, channels), jnp.bfloat16),
+            jax.ShapeDtypeStruct((residues, pair_channels), jnp.bfloat16),
+            weight,
+            weight,
+            weight,
+            weight,
+            jax.ShapeDtypeStruct((span, channels), jnp.float32),
+            jax.ShapeDtypeStruct((HEAD_NUMBER, pair_channels), jnp.float32),
+            jax.ShapeDtypeStruct((1, channels), jnp.float32),
+            jax.ShapeDtypeStruct((1, pair_channels), jnp.float32),
+        ),
+        in_specs=[vmem] * 9,
+        out_specs=(vmem,) * 11,
+        scratch_shapes=[pltpu.VMEM((residues, residues, pair_channels), jnp.bfloat16)],
+        compiler_params=pltpu.CompilerParams(vmem_limit_bytes=32 * 1024 * 1024),
+        name="whole_part",
+    )(
+        gathered,
+        alignment_scaling_factor.reshape(1, channels),
+        couple_scaling_factor.reshape(1, pair_channels),
+        request_matrix,
+        lookup_matrix,
+        content_matrix,
+        switch_matrix,
+        final_projection_matrix,
+        couple_to_headterm_matrix,
+    )
+    return (
+        outs[0].reshape(alignment_embedding.shape),
+        outs[1].reshape(alignment_embedding.shape),
+        outs[2].reshape(couple_embedding.shape),
+        *outs[3:8],
+        outs[8].T,
+        outs[9].reshape(channels),
+        outs[10].reshape(pair_channels),
+    )
+
+
 def on_device(
     alignment_embedding,
     alignment_existing_flags,
@@ -195,6 +576,21 @@
     couple_to_headterm_matrix,
     increment_adjoint,
 ):
+    if whole_part_fits(alignment_embedding, couple_embedding):
+        return on_device_whole_part(
+            alignment_embedding,
+            alignment_existing_flags,
+            couple_embedding,
+            alignment_scaling_factor,
+            couple_scaling_factor,
+            request_matrix,
+            lookup_matrix,
+            content_matrix,
+            switch_matrix,
+            final_projection_matrix,
+            couple_to_headterm_matrix,
+            increment_adjoint,
+        )
     filter_shared = alignment_existing_flags.astype(jnp.bfloat16)
     alignment_line_embedding, alignment_line_flags = (
         lax.all_to_all(alignment_embedding, "dap", split_axis=0, concat_axis=1, tiled=True),

time: 244 us -> 23.8 us (0.10)
  blocking collectives: 119 us -> 0 us
  waiting for transfers between devices: 59.1 us -> 0 us
  starting transfers between devices: 21.4 us -> 0 us
  Pallas kernels: 0 us -> 18.6 us
  between operations: 14.3 us -> 0.74 us
  local copies, waits for them, and re-layouts: 14.6 us -> 4.28 us
  matrix products: 9.75 us -> 0 us
  other arithmetic: 5.37 us -> 0 us
    unnamed x1 -> x0, blocking collectives: 61.9 us -> none
    psum x1 -> x0, waiting for transfers between devices: 49.7 us -> none  [on_device(): lax.psum((subtotal_list[0], subtotal_list[1], subtotal_list[2], subtotal_...]
    psum x1 -> x0, blocking collectives: 35.1 us -> none  [on_device(): lax.psum((subtotal_list[0], subtotal_list[1], subtotal_list[2], subtotal_...]
    all_gather x1 -> x0, blocking collectives: 21.8 us -> none  [on_device(): couple_headwise_terms = lax.all_gather(bias_rows, 'dap', axis=0, tiled=True)]
    all_to_all x5 -> x0, starting transfers between devices: 21.4 us -> none  [the longest x1 7.39 us: on_device(): lax.all_to_all(filter_shared, 'dap', split_axis=0, concat_axis=1, tiled=T...]
    pallas_call x0 -> x2, Pallas kernels: none -> 18.6 us  [the longest x1 14.3 us: on_device_whole_part(): pl.pallas_call(lambda *refs: gather_kernel(devices, *refs), out_shape=jax...]
    dot_general x24 -> x0, matrix products: 9.75 us -> none  [the longest x5 4.99 us: tensor_product(): lax.dot_general(left, right, (((0,), (0,)), ((), ())), preferred_element_...]
    all_to_all x5 -> x0, waiting for transfers between devices: 9.37 us -> none  [the longest x1 6.09 us: on_device(): lax.all_to_all(alignment_embedding, 'dap', split_axis=0, concat_axis=1, t...]
  transfers between devices with their start and end apart: 6 -> 0, of which waited for: 3 -> 0; matrix products, arithmetic and copies ran while one was open for 6% -> 0% of each run, Pallas kernels for 0% -> 0%
where the time goes in v1:
time: 23.8 us; the launch traced here: 23.6 us
  Pallas kernels  18.6 us (78%)
  local copies, waits for them, and re-layouts  4.28 us (18%)
  between operations  0.74 us (3%)
    pallas_call x1, Pallas kernels, on_device_whole_part(): pl.pallas_call(lambda *refs: gather_kernel(devices, *refs), out_shape=jax...  14.3 us
    unnamed x22, local copies, waits for them, and re-layouts  4.28 us
    pallas_call x1, Pallas kernels, on_device_whole_part(): pl.pallas_call(part_kernel, out_shape=(jax.ShapeDtypeStruct((sequences, c...  4.26 us

profile of v1, /device:TPU:0, one launch (start us, length us, event | category | flops | bytes accessed | tf_op | source)
XLA Modules:
  0.0 23.6 jit_solution(4579782187395527019)
XLA Ops:
  0.6 0.0 copy-start.9
  0.7 0.6 %copy-done.9 = s32[16,1]{0,1:T(1,128)S(1)} copy-done((s32[16,1]{0,1:T(1,128)S(1)}, s32[16,1]{0,1:T(1,128)}, u32[]{:S(2)}) %copy-start.9) | copy-done | bytes 88
  1.3 0.0 copy-start.8
  1.3 0.7 %copy.23.refs_1_ = s32[16,1]{1,0:T(8,128)} copy(s32[16,1]{0,1:T(1,128)S(1)} %copy-done.9) | data formatting | bytes 128 | tf_op args[1]
  2.0 0.0 copy-done.8
  2.0 0.1 copy.24.headterm_ref
  2.1 0.0 copy-start.1
  2.1 0.0 copy-start.2
  2.1 0.0 copy-start.3
  2.1 0.0 copy-start.6
  2.1 0.0 copy-start.7
  2.2 14.3 %gather_part.1.all_ref = bf16[16,48,256]{2,1,0:T(8,128)(2,1)} custom-call(bf16[16,256]{1,0:T(8,128)(2,1)} %bitcast.13, s32[16,1]{1,0:T(8,128)} %copy.23.refs_1_, bf16[16,128]{1,0:T(8,128)(2,1)} %bitcast.15, bf16[16,256]{1,0:T(8,128)(2,1)} %bitcast.14), custom_call_target="tpu_custom_call" | custom-call | tf_op jit(solution)/shard_map/gather_part/pallas_call | solution.py:504
  16.5 0.0 copy-done.1
  16.5 0.0 copy-done.2
  16.5 0.0 copy-done.3
  16.5 0.0 copy-done.6
  16.5 0.0 copy-done.7
  16.5 0.0 copy-start
  16.5 1.0 %copy-done = bf16[16,48,256]{2,1,0:T(8,128)(2,1)S(1)} copy-done((bf16[16,48,256]{2,1,0:T(8,128)(2,1)S(1)}, bf16[16,48,256]{2,1,0:T(8,128)(2,1)}, u32[]{:S(2)}) %copy-start) | copy-done | bytes 393240
  17.5 0.0 copy-start.4
  17.5 0.9 %copy-done.4 = bf16[256,256]{1,0:T(8,128)(2,1)S(1)} copy-done((bf16[256,256]{1,0:T(8,128)(2,1)S(1)}, bf16[256,256]{1,0:T(8,128)(2,1)}, u32[]{:S(2)}) %copy-start.4) | copy-done | bytes 131096
  18.4 0.0 copy-start.5
  18.4 0.9 %copy-done.5 = bf16[256,256]{1,0:T(8,128)(2,1)S(1)} copy-done((bf16[256,256]{1,0:T(8,128)(2,1)S(1)}, bf16[256,256]{1,0:T(8,128)(2,1)}, u32[]{:S(2)}) %copy-start.5) | copy-done | bytes 131096
  19.3 4.3 %whole_part.1 = (bf16[16,256]{1,0:T(8,128)(2,1)}, bf16[16,256]{1,0:T(8,128)(2,1)}, bf16[16,128]{1,0:T(8,128)(2,1)}, f32[256,256]{1,0:T(8,128)}, f32[256,256]{1,0...) custom-call(bf16[16,48,256]{2,1,0:T(8,128)(2,1)S(1)} %copy-done, ...), custom_call_target="tpu_custom_call" | custom-call | tf_op jit(solution)/shard_map/whole_part/pallas_call | solution.py:523
Async XLA Ops:
  0.6 0.7 %copy-start.9 = (s32[16,1]{0,1:T(1,128)S(1)}, s32[16,1]{0,1:T(1,128)}, u32[]{:S(2)}) copy-start(s32[16,1]{0,1:T(1,128)} %param.13) | copy-start | bytes 196
  1.3 0.7 %copy-start.8 = (bf16[128,8]{0,1:T(8,128)(2,1)S(1)}, bf16[128,8]{0,1:T(8,128)(2,1)}, u32[]{:S(2)}) copy-start(bf16[128,8]{0,1:T(8,128)(2,1)} %param.22) | copy-start | bytes 6148
  2.1 14.4 %copy-start.1 = (bf16[256,256]{1,0:T(8,128)(2,1)S(1)}, bf16[256,256]{1,0:T(8,128)(2,1)}, u32[]{:S(2)}) copy-start(bf16[256,256]{1,0:T(8,128)(2,1)} %request_ref.1) | copy-start | bytes 393220
  2.1 14.4 %copy-start.2 = (bf16[256,256]{1,0:T(8,128)(2,1)S(1)}, bf16[256,256]{1,0:T(8,128)(2,1)}, u32[]{:S(2)}) copy-start(bf16[256,256]{1,0:T(8,128)(2,1)} %lookup_ref.1) | copy-start | bytes 393220
  2.1 14.4 %copy-start.3 = (bf16[256,256]{1,0:T(8,128)(2,1)S(1)}, bf16[256,256]{1,0:T(8,128)(2,1)}, u32[]{:S(2)}) copy-start(bf16[256,256]{1,0:T(8,128)(2,1)} %content_ref.1) | copy-start | bytes 393220
  2.1 14.4 %copy-start.6 = (f32[256]{0:T(256)S(1)}, f32[256]{0:T(256)}, u32[]{:S(2)}) copy-start(f32[256]{0:T(256)} %param.15) | copy-start | bytes 3076
  2.1 14.4 %copy-start.7 = (f32[128]{0:T(128)S(1)}, f32[128]{0:T(128)}, u32[]{:S(2)}) copy-start(f32[128]{0:T(128)} %param.16) | copy-start | bytes 1540
  16.5 1.0 %copy-start = (bf16[16,48,256]{2,1,0:T(8,128)(2,1)S(1)}, bf16[16,48,256]{2,1,0:T(8,128)(2,1)}, u32[]{:S(2)}) copy-start(bf16[16,48,256]{2,1,0:T(8,128)(2,1)} %gather_part.1.all_ref) | copy-start | bytes 1179652
  17.5 0.9 %copy-start.4 = (bf16[256,256]{1,0:T(8,128)(2,1)S(1)}, bf16[256,256]{1,0:T(8,128)(2,1)}, u32[]{:S(2)}) copy-start(bf16[256,256]{1,0:T(8,128)(2,1)} %switch_ref.1) | copy-start | bytes 393220
  18.4 0.9 %copy-start.5 = (bf16[256,256]{1,0:T(8,128)(2,1)S(1)}, bf16[256,256]{1,0:T(8,128)(2,1)}, u32[]{:S(2)}) copy-start(bf16[256,256]{1,0:T(8,128)(2,1)} %final_ref.1) | copy-start | bytes 393220

commit v2 on v1

--- a/solution.py
+++ b/solution.py
@@ -223,8 +223,9 @@
     all_ref[me, 0:rows, :] = msa_ref[...]
     all_ref[me, rows : 2 * rows, :] = grad_ref[...]
     all_ref[me, 2 * rows :, 0:lanes] = pair_ref[...]
-    all_ref[me, 2 * rows :, lanes:] = jnp.broadcast_to(
-        flag_ref[...].astype(jnp.float32), (rows, lanes)
+    flags = jnp.broadcast_to(flag_ref[...].astype(jnp.float32), (rows, rows))
+    all_ref[me, 2 * rows :, lanes:] = jnp.concatenate(
+        [flags, jnp.zeros((rows, lanes - rows), jnp.float32)], axis=1
     ).astype(jnp.bfloat16)
     pl.semaphore_wait(barrier, planes + 1)
 
@@ -355,7 +356,7 @@
     spread = one_where(
         iota((HEAD_NUMBER, columns), 0) == iota((HEAD_NUMBER, columns), 1) // residues
     )
-    headterm_wide = product(headterm_ref[...], spread).astype(jnp.bfloat16)
+    headterm_wide = product(headterm_ref[...], spread, INNER).astype(jnp.bfloat16)
     pair_shape = (residues * residues, columns)
     same_key = iota(pair_shape, 0) % residues == iota(pair_shape, 1) % residues
     bias = jnp.sum(
@@ -366,13 +367,11 @@
     )
     bias = bias.astype(jnp.bfloat16).astype(jnp.float32)
 
-    flag_lane = iota((sequences, columns), 1) % residues
-    flags = jnp.zeros((sequences, columns), jnp.float32)
-    for j in range(residues):
-        flags = jnp.where(
-            flag_lane == j, all_ref[j, 2 * sequences :, pair_lanes:].astype(jnp.float32), flags
-        )
-    fill = 1000000000.0 * (flags - 1.0)
+    flags = all_ref[:, 2 * sequences :, pair_lanes:].astype(jnp.float32)
+    flags = flags[:, 0, :].astype(jnp.bfloat16)
+    key_shape = (residues, columns)
+    flags = product(flags, one_where(iota(key_shape, 0) == iota(key_shape, 1) % residues), INNER)
+    fill = 1000000000.0 * (flags[0:sequences] - 1.0)
 
     square = (tokens, tokens)
     reorder = one_where(
@@ -510,11 +509,16 @@
             pltpu.SemaphoreType.DMA((devices - 1,)),
             pltpu.SemaphoreType.DMA((devices,)),
         ],
-        compiler_params=pltpu.CompilerParams(collective_id=0, has_side_effects=True),
+        compiler_params=pltpu.CompilerParams(
+            collective_id=0, has_side_effects=True, vmem_limit_bytes=8 * 1024 * 1024
+        ),
+        cost_estimate=pl.CostEstimate(
+            flops=0, bytes_accessed=100 * devices * 3 * sequences * channels * 2, transcendentals=0
+        ),
         name="gather_part",
     )(
         alignment_embedding.reshape(sequences, channels),
-        alignment_existing_flags,
+        alignment_existing_flags.T,
         couple_embedding.reshape(residues, pair_channels),
         increment_adjoint.reshape(sequences, channels),
     )
@@ -538,7 +542,7 @@
         in_specs=[vmem] * 9,
         out_specs=(vmem,) * 11,
         scratch_shapes=[pltpu.VMEM((residues, residues, pair_channels), jnp.bfloat16)],
-        compiler_params=pltpu.CompilerParams(vmem_limit_bytes=32 * 1024 * 1024),
+        compiler_params=pltpu.CompilerParams(vmem_limit_bytes=24 * 1024 * 1024),
         name="whole_part",
     )(
         gathered,
@@ -549,7 +553,7 @@
         content_matrix,
         switch_matrix,
         final_projection_matrix,
-        couple_to_headterm_matrix,
+        couple_to_headterm_matrix.T,
     )
     return (
         outs[0].reshape(alignment_embedding.shape),

time: 23.8 us -> 21.3 us (0.89)
  Pallas kernels: 18.6 us -> 17.1 us
  local copies, waits for them, and re-layouts: 4.28 us -> 3.2 us
    pallas_call x1, Pallas kernels: 14.3 us -> 12.8 us  [on_device_whole_part(): pl.pallas_call(lambda *refs: gather_kernel(devices, *refs), out_shape=jax...]
    unnamed x22 -> x24, local copies, waits for them, and re-layouts: 4.28 us -> 3.2 us
where the time goes in v2:
time: 21.3 us; the launch traced here: 21 us
  Pallas kernels  17.1 us (80%)
  local copies, waits for them, and re-layouts  3.2 us (15%)
  between operations  0.76 us (4%)
    pallas_call x1, Pallas kernels, on_device_whole_part(): pl.pallas_call(lambda *refs: gather_kernel(devices, *refs), out_shape=jax...  12.8 us
    pallas_call x1, Pallas kernels, on_device_whole_part(): pl.pallas_call(part_kernel, out_shape=(jax.ShapeDtypeStruct((sequences, c...  4.3 us
    unnamed x24, local copies, waits for them, and re-layouts  3.2 us

profile of v2, /device:TPU:0, one launch (start us, length us, event | category | flops | bytes accessed | tf_op | source)
XLA Modules:
  0.0 21.0 jit_solution(8303010053480854217)
XLA Ops:
  0.6 0.0 copy-start.5
  0.7 0.0 copy-start.7
  0.7 0.0 copy-start.10
  0.7 0.7 %copy-done.5 = bf16[16,1,256]{2,0,1:T(8,128)(2,1)S(1)} copy-done((bf16[16,1,256]{2,0,1:T(8,128)(2,1)S(1)}, bf16[16,1,256]{2,0,1:T(8,128)(2,1)}, u32[]{:S(2)}) %copy-start.5) | copy-done | bytes 8216
  1.3 0.0 copy-done.7
  1.4 0.0 copy-done.10
  1.4 0.0 copy-start.6
  1.4 0.7 %copy-done.6 = bf16[16,1,256]{2,0,1:T(8,128)(2,1)S(1)} copy-done((bf16[16,1,256]{2,0,1:T(8,128)(2,1)S(1)}, bf16[16,1,256]{2,0,1:T(8,128)(2,1)}, u32[]{:S(2)}) %copy-start.6) | copy-done | bytes 8216
  2.1 0.0 copy-start
  2.1 0.0 copy-start.1
  2.1 0.0 copy-start.2
  2.1 0.0 copy-start.8
  2.1 0.0 copy-start.9
  2.1 0.0 copy-start.11
  2.1 12.8 %gather_part.1.all_ref = bf16[16,48,256]{2,1,0:T(8,128)(2,1)S(1)} custom-call(bf16[16,256]{1,0:T(8,128)(2,1)S(1)} %bitcast.13, s32[1,16]{1,0:T(1,128)S(1)} %bitcast.18, bf16[16,128]{1,0:T(8,128)(2,1)S(1)} %bitcast.15, bf16[16,256]{1,0:T(8,128)(2,1)S(1)} %bitcast.14), custom_call_target="tpu_custom_call" | custom-call | bytes 39321600 | tf_op jit(solution)/shard_map/gather_part/pallas_call | solution.py:503
  14.9 0.0 copy-done
  14.9 0.0 copy-done.1
  14.9 0.0 copy-done.2
  14.9 0.0 copy-done.8
  14.9 0.0 copy-done.9
  14.9 0.0 copy-done.11
  14.9 0.0 copy-start.3
  14.9 0.9 %copy-done.3 = bf16[256,256]{1,0:T(8,128)(2,1)S(1)} copy-done((bf16[256,256]{1,0:T(8,128)(2,1)S(1)}, bf16[256,256]{1,0:T(8,128)(2,1)}, u32[]{:S(2)}) %copy-start.3) | copy-done | bytes 131096
  15.8 0.0 copy-start.4
  15.8 0.9 %copy-done.4 = bf16[256,256]{1,0:T(8,128)(2,1)S(1)} copy-done((bf16[256,256]{1,0:T(8,128)(2,1)S(1)}, bf16[256,256]{1,0:T(8,128)(2,1)}, u32[]{:S(2)}) %copy-start.4) | copy-done | bytes 131096
  16.7 4.3 %whole_part.1 = (bf16[16,256]{1,0:T(8,128)(2,1)}, bf16[16,256]{1,0:T(8,128)(2,1)}, bf16[16,128]{1,0:T(8,128)(2,1)}, f32[256,256]{1,0:T(8,128)}, f32[256,256]{1,0...) custom-call(bf16[16,48,256]{2,1,0:T(8,128)(2,1)S(1)} %gather_part.1., ...), custom_call_target="tpu_custom_call" | custom-call | tf_op jit(solution)/shard_map/whole_part/pallas_call | solution.py:527
Async XLA Ops:
  0.6 0.7 %copy-start.5 = (bf16[16,1,256]{2,0,1:T(8,128)(2,1)S(1)}, bf16[16,1,256]{2,0,1:T(8,128)(2,1)}, u32[]{:S(2)}) copy-start(bf16[16,1,256]{2,0,1:T(8,128)(2,1)} %param.12) | copy-start | bytes 24580
  0.7 0.7 %copy-start.7 = (bf16[1,16,128]{2,1,0:T(8,128)(2,1)S(1)}, bf16[1,16,128]{2,1,0:T(8,128)(2,1)}, u32[]{:S(2)}) copy-start(bf16[1,16,128]{2,1,0:T(8,128)(2,1)} %param.14) | copy-start | bytes 12292
  0.7 0.7 %copy-start.10 = (s32[16,1]{0,1:T(1,128)S(1)}, s32[16,1]{0,1:T(1,128)}, u32[]{:S(2)}) copy-start(s32[16,1]{0,1:T(1,128)} %param.13) | copy-start | bytes 196
  1.4 0.7 %copy-start.6 = (bf16[16,1,256]{2,0,1:T(8,128)(2,1)S(1)}, bf16[16,1,256]{2,0,1:T(8,128)(2,1)}, u32[]{:S(2)}) copy-start(bf16[16,1,256]{2,0,1:T(8,128)(2,1)} %param.23) | copy-start | bytes 24580
  2.1 12.8 %copy-start = (bf16[256,256]{1,0:T(8,128)(2,1)S(1)}, bf16[256,256]{1,0:T(8,128)(2,1)}, u32[]{:S(2)}) copy-start(bf16[256,256]{1,0:T(8,128)(2,1)} %request_ref.1) | copy-start | bytes 393220
  2.1 12.8 %copy-start.1 = (bf16[256,256]{1,0:T(8,128)(2,1)S(1)}, bf16[256,256]{1,0:T(8,128)(2,1)}, u32[]{:S(2)}) copy-start(bf16[256,256]{1,0:T(8,128)(2,1)} %lookup_ref.1) | copy-start | bytes 393220
  2.1 12.8 %copy-start.2 = (bf16[256,256]{1,0:T(8,128)(2,1)S(1)}, bf16[256,256]{1,0:T(8,128)(2,1)}, u32[]{:S(2)}) copy-start(bf16[256,256]{1,0:T(8,128)(2,1)} %content_ref.1) | copy-start | bytes 393220
  2.1 12.8 %copy-start.8 = (bf16[128,8]{0,1:T(8,128)(2,1)S(1)}, bf16[128,8]{0,1:T(8,128)(2,1)}, u32[]{:S(2)}) copy-start(bf16[128,8]{0,1:T(8,128)(2,1)} %param.22) | copy-start | bytes 6148
  2.1 12.8 %copy-start.9 = (f32[256]{0:T(256)S(1)}, f32[256]{0:T(256)}, u32[]{:S(2)}) copy-start(f32[256]{0:T(256)} %param.15) | copy-start | bytes 3076
  2.1 12.8 %copy-start.11 = (f32[128]{0:T(128)S(1)}, f32[128]{0:T(128)}, u32[]{:S(2)}) copy-start(f32[128]{0:T(128)} %param.16) | copy-start | bytes 1540
  14.9 0.9 %copy-start.3 = (bf16[256,256]{1,0:T(8,128)(2,1)S(1)}, bf16[256,256]{1,0:T(8,128)(2,1)}, u32[]{:S(2)}) copy-start(bf16[256,256]{1,0:T(8,128)(2,1)} %switch_ref.1) | copy-start | bytes 393220
  15.8 0.9 %copy-start.4 = (bf16[256,256]{1,0:T(8,128)(2,1)S(1)}, bf16[256,256]{1,0:T(8,128)(2,1)}, u32[]{:S(2)}) copy-start(bf16[256,256]{1,0:T(8,128)(2,1)} %final_ref.1) | copy-start | bytes 393220

commit v3 on v2

--- a/solution.py
+++ b/solution.py
@@ -203,31 +203,25 @@
     )
 
 
-def gather_kernel(devices, msa_ref, flag_ref, pair_ref, grad_ref, all_ref, send_sem, recv_sem):
+def gather_kernel(devices, block_ref, all_ref, send_sem, recv_sem):
     me = lax.axis_index("dap")
-    rows = msa_ref.shape[0]
-    lanes = pair_ref.shape[1]
     planes = devices // 4
-    core = lax.rem(me, 2)
-    row = lax.rem(me // 2, 2)
+    place = lax.rem(me, 4)
+    core = lax.rem(place, 2)
+    row = place // 2
     sibling = me + 1 - 2 * core
     across = me + 2 - 4 * row
+    opposite = me + 3 - 2 * place
+    beside = [across, opposite, sibling]
     far = [lax.rem(me + 4 * k, devices) for k in range(1, planes)]
-    far_across = [lax.rem(across + 4 * k, devices) for k in range(1, planes)]
 
     barrier = pltpu.get_barrier_semaphore()
-    for peer in far + [across, sibling]:
+    for peer in far + beside:
         pl.semaphore_signal(
             barrier, inc=1, device_id={"dap": peer}, device_id_type=pl.DeviceIdType.MESH
         )
-    all_ref[me, 0:rows, :] = msa_ref[...]
-    all_ref[me, rows : 2 * rows, :] = grad_ref[...]
-    all_ref[me, 2 * rows :, 0:lanes] = pair_ref[...]
-    flags = jnp.broadcast_to(flag_ref[...].astype(jnp.float32), (rows, rows))
-    all_ref[me, 2 * rows :, lanes:] = jnp.concatenate(
-        [flags, jnp.zeros((rows, lanes - rows), jnp.float32)], axis=1
-    ).astype(jnp.bfloat16)
-    pl.semaphore_wait(barrier, planes + 1)
+    all_ref[me] = block_ref[...]
+    pl.semaphore_wait(barrier, planes + 2)
 
     sent = []
 
@@ -253,23 +247,15 @@
             device_id_type=pl.DeviceIdType.MESH,
         ).wait_recv()
 
-    for peer in far:
+    for peer in far + beside:
         send(me, peer)
-    send(me, across)
-    send(me, sibling)
-    arrive(across)
-    send(across, sibling)
     for slot in far:
         arrive(slot)
-        send(slot, across)
-        send(slot, sibling)
-    for slot in far_across:
-        arrive(slot)
-        send(slot, sibling)
-    sibling_across = sibling + 2 - 4 * row
-    for k in range(planes):
-        arrive(lax.rem(sibling + 4 * k, devices))
-        arrive(lax.rem(sibling_across + 4 * k, devices))
+        for peer in beside:
+            send(slot, peer)
+    for first in beside:
+        for k in range(planes):
+            arrive(lax.rem(first + 4 * k, devices))
     for copy in sent:
         copy.wait_send()
 
@@ -500,10 +486,28 @@
     _, residues, pair_channels = couple_embedding.shape
     devices = lax.axis_size("dap")
     vmem = pl.BlockSpec(memory_space=pltpu.VMEM)
+    flags = jnp.pad(
+        alignment_existing_flags.T.astype(jnp.bfloat16),
+        ((0, 0), (0, channels - pair_channels - sequences)),
+    )
+    block = jnp.concatenate(
+        [
+            alignment_embedding.reshape(sequences, channels),
+            increment_adjoint.reshape(sequences, channels),
+            jnp.concatenate(
+                [
+                    couple_embedding.reshape(residues, pair_channels),
+                    jnp.broadcast_to(flags, (residues, channels - pair_channels)),
+                ],
+                axis=1,
+            ),
+        ],
+        axis=0,
+    )
     gathered = pl.pallas_call(
         lambda *refs: gather_kernel(devices, *refs),
-        out_shape=jax.ShapeDtypeStruct((devices, 3 * sequences, channels), jnp.bfloat16),
-        in_specs=[vmem] * 4,
+        out_shape=jax.ShapeDtypeStruct((devices, *block.shape), jnp.bfloat16),
+        in_specs=[vmem],
         out_specs=vmem,
         scratch_shapes=[
             pltpu.SemaphoreType.DMA((devices - 1,)),
@@ -513,15 +517,10 @@
             collective_id=0, has_side_effects=True, vmem_limit_bytes=8 * 1024 * 1024
         ),
         cost_estimate=pl.CostEstimate(
-            flops=0, bytes_accessed=100 * devices * 3 * sequences * channels * 2, transcendentals=0
+            flops=0, bytes_accessed=100 * devices * block.size * 2, transcendentals=0
         ),
         name="gather_part",
-    )(
-        alignment_embedding.reshape(sequences, channels),
-        alignment_existing_flags.T,
-        couple_embedding.reshape(residues, pair_channels),
-        increment_adjoint.reshape(sequences, channels),
-    )
+    )(block)
     span = HEAD_NUMBER * HEAD_DIMENSION
     weight = jax.ShapeDtypeStruct((channels, span), jnp.float32)
     outs = pl.pallas_call(

time: 21.3 us -> 21.2 us (level)
  other arithmetic: 0 us -> 0.69 us
  local copies, waits for them, and re-layouts: 3.2 us -> 2.53 us
    concatenate x0 -> x1, other arithmetic: none -> 0.69 us  [on_device_whole_part(): jnp.concatenate([alignment_embedding.reshape(sequences, channels), increm...]
    unnamed x24 -> x22, local copies, waits for them, and re-layouts: 3.2 us -> 2.52 us
where the time goes in v3:
time: 21.2 us; the launch traced here: 20.9 us
  Pallas kernels  16.9 us (80%)
  local copies, waits for them, and re-layouts  2.53 us (12%)
  between operations  0.76 us (4%)
  other arithmetic  0.69 us (3%)
    pallas_call x1, Pallas kernels, on_device_whole_part(): pl.pallas_call(lambda *refs: gather_kernel(devices, *refs), out_shape=jax...  12.6 us
    pallas_call x1, Pallas kernels, on_device_whole_part(): pl.pallas_call(part_kernel, out_shape=(jax.ShapeDtypeStruct((sequences, c...  4.3 us
    unnamed x22, local copies, waits for them, and re-layouts  2.52 us
    concatenate x1, other arithmetic, on_device_whole_part(): jnp.concatenate([alignment_embedding.reshape(sequences, channels), increm...  0.69 us

profile of v3, /device:TPU:0, one launch (start us, length us, event | category | flops | bytes accessed | tf_op | source)
XLA Modules:
  0.0 20.9 jit_solution(13621128038828052592)
XLA Ops:
  0.6 0.0 copy-start.10
  0.7 0.0 copy-start.9
  0.7 0.0 copy-start.8
  0.7 0.6 %copy-done.10 = s32[16,1]{0,1:T(1,128)S(1)} copy-done((s32[16,1]{0,1:T(1,128)S(1)}, s32[16,1]{0,1:T(1,128)}, u32[]{:S(2)}) %copy-start.10) | copy-done | bytes 88
  1.3 0.0 copy-done.9
  1.4 0.0 copy-done.8
  1.4 0.7 %maximum_maximum_fusion.refs_0_ = bf16[48,256]{1,0:T(8,128)(2,1)S(1)} fusion(bf16[16,128]{1,0:T(8,128)(2,1)S(1)} %broadcast_in_dim.8, bf16[16,128]{1,0:T(8,128)(2,1)} %bitcast.21, bf16[16,256]{1,0:T(8,128)(2,1)S(1)} %bitcast.19, bf16[16,256]{1,0:T(8,128)(2,1)S(1)} %bitcast.20), kind=kLoop, calls=%fused_computation | loop fusion | flops 98304 | bytes 49152 | tf_op jit(solution)/shard_map/concatenate | solution.py:493
  2.1 0.0 copy-start
  2.1 0.0 copy-start.1
  2.1 0.0 copy-start.2
  2.1 0.0 copy-start.5
  2.1 0.0 copy-start.6
  2.1 0.0 copy-start.7
  2.1 12.6 %gather_part.1.all_ref = bf16[16,48,256]{2,1,0:T(8,128)(2,1)S(1)} custom-call(bf16[48,256]{1,0:T(8,128)(2,1)S(1)} %maximum_maximum_fusion.refs_0_), custom_call_target="tpu_custom_call" | custom-call | bytes 39321600 | tf_op jit(solution)/shard_map/gather_part/pallas_call | solution.py:507
  14.7 0.0 copy-done
  14.8 0.0 copy-done.1
  14.8 0.0 copy-done.2
  14.8 0.0 copy-done.5
  14.8 0.0 copy-done.6
  14.8 0.0 copy-done.7
  14.8 0.0 copy-start.3
  14.8 0.9 %copy-done.3 = bf16[256,256]{1,0:T(8,128)(2,1)S(1)} copy-done((bf16[256,256]{1,0:T(8,128)(2,1)S(1)}, bf16[256,256]{1,0:T(8,128)(2,1)}, u32[]{:S(2)}) %copy-start.3) | copy-done | bytes 131096
  15.7 0.0 copy-start.4
  15.7 0.9 %copy-done.4 = bf16[256,256]{1,0:T(8,128)(2,1)S(1)} copy-done((bf16[256,256]{1,0:T(8,128)(2,1)S(1)}, bf16[256,256]{1,0:T(8,128)(2,1)}, u32[]{:S(2)}) %copy-start.4) | copy-done | bytes 131096
  16.6 4.3 %whole_part.1 = (bf16[16,256]{1,0:T(8,128)(2,1)}, bf16[16,256]{1,0:T(8,128)(2,1)}, bf16[16,128]{1,0:T(8,128)(2,1)}, f32[256,256]{1,0:T(8,128)}, f32[256,256]{1,0...) custom-call(bf16[16,48,256]{2,1,0:T(8,128)(2,1)S(1)} %gather_part.1., ...), custom_call_target="tpu_custom_call" | custom-call | tf_op jit(solution)/shard_map/whole_part/pallas_call | solution.py:526
  (3 shorter events, 0.0 us)
Async XLA Ops:
  0.6 0.7 %copy-start.10 = (s32[16,1]{0,1:T(1,128)S(1)}, s32[16,1]{0,1:T(1,128)}, u32[]{:S(2)}) copy-start(s32[16,1]{0,1:T(1,128)} %param.13) | copy-start | bytes 196
  0.7 0.7 %copy-start.9 = (bf16[16,1,256]{2,0,1:T(8,128)(2,1)S(1)}, bf16[16,1,256]{2,0,1:T(8,128)(2,1)}, u32[]{:S(2)}) copy-start(bf16[16,1,256]{2,0,1:T(8,128)(2,1)} %param.12) | copy-start | bytes 24580
  0.7 0.7 %copy-start.8 = (bf16[16,1,256]{2,0,1:T(8,128)(2,1)S(1)}, bf16[16,1,256]{2,0,1:T(8,128)(2,1)}, u32[]{:S(2)}) copy-start(bf16[16,1,256]{2,0,1:T(8,128)(2,1)} %param.23) | copy-start | bytes 24580
  2.1 12.7 %copy-start = (bf16[256,256]{1,0:T(8,128)(2,1)S(1)}, bf16[256,256]{1,0:T(8,128)(2,1)}, u32[]{:S(2)}) copy-start(bf16[256,256]{1,0:T(8,128)(2,1)} %request_ref.1) | copy-start | bytes 393220
  2.1 12.7 %copy-start.1 = (bf16[256,256]{1,0:T(8,128)(2,1)S(1)}, bf16[256,256]{1,0:T(8,128)(2,1)}, u32[]{:S(2)}) copy-start(bf16[256,256]{1,0:T(8,128)(2,1)} %lookup_ref.1) | copy-start | bytes 393220
  2.1 12.7 %copy-start.2 = (bf16[256,256]{1,0:T(8,128)(2,1)S(1)}, bf16[256,256]{1,0:T(8,128)(2,1)}, u32[]{:S(2)}) copy-start(bf16[256,256]{1,0:T(8,128)(2,1)} %content_ref.1) | copy-start | bytes 393220
  2.1 12.7 %copy-start.5 = (bf16[128,8]{0,1:T(8,128)(2,1)S(1)}, bf16[128,8]{0,1:T(8,128)(2,1)}, u32[]{:S(2)}) copy-start(bf16[128,8]{0,1:T(8,128)(2,1)} %param.22) | copy-start | bytes 6148
  2.1 12.7 %copy-start.6 = (f32[256]{0:T(256)S(1)}, f32[256]{0:T(256)}, u32[]{:S(2)}) copy-start(f32[256]{0:T(256)} %param.15) | copy-start | bytes 3076
  2.1 12.7 %copy-start.7 = (f32[128]{0:T(128)S(1)}, f32[128]{0:T(128)}, u32[]{:S(2)}) copy-start(f32[128]{0:T(128)} %param.16) | copy-start | bytes 1540
  14.8 0.9 %copy-start.3 = (bf16[256,256]{1,0:T(8,128)(2,1)S(1)}, bf16[256,256]{1,0:T(8,128)(2,1)}, u32[]{:S(2)}) copy-start(bf16[256,256]{1,0:T(8,128)(2,1)} %switch_ref.1) | copy-start | bytes 393220
  15.7 0.9 %copy-start.4 = (bf16[256,256]{1,0:T(8,128)(2,1)S(1)}, bf16[256,256]{1,0:T(8,128)(2,1)}, u32[]{:S(2)}) copy-start(bf16[256,256]{1,0:T(8,128)(2,1)} %final_ref.1) | copy-start | bytes 393220

commit v4 on v3

--- a/solution.py
+++ b/solution.py
@@ -195,7 +195,7 @@
         owned == 1
         and owned_pairs == 1
         and devices == residues
-        and devices % 4 == 0
+        and devices % 8 == 0
         and HEAD_NUMBER * residues == LANES
         and pair_channels == LANES
         and sequences == residues
@@ -203,7 +203,8 @@
     )
 
 
-def gather_kernel(devices, block_ref, all_ref, send_sem, recv_sem):
+def gather_kernel(devices, msa_ref, grad_ref, pair_ref, all_ref, send_sem, recv_sem):
+    rows = msa_ref.shape[0]
     me = lax.axis_index("dap")
     planes = devices // 4
     place = lax.rem(me, 4)
@@ -214,14 +215,18 @@
     opposite = me + 3 - 2 * place
     beside = [across, opposite, sibling]
     far = [lax.rem(me + 4 * k, devices) for k in range(1, planes)]
+    far_across = [lax.rem(across + 4 * k, devices) for k in range(1, planes)]
+    direct = far + far_across[0::2]
 
     barrier = pltpu.get_barrier_semaphore()
-    for peer in far + beside:
+    for peer in direct + beside:
         pl.semaphore_signal(
             barrier, inc=1, device_id={"dap": peer}, device_id_type=pl.DeviceIdType.MESH
         )
-    all_ref[me] = block_ref[...]
-    pl.semaphore_wait(barrier, planes + 2)
+    all_ref[me, 0:rows, :] = msa_ref[...]
+    all_ref[me, rows : 2 * rows, :] = grad_ref[...]
+    all_ref[me, 2 * rows :, :] = pair_ref[...]
+    pl.semaphore_wait(barrier, len(direct) + len(beside))
 
     sent = []
 
@@ -247,15 +252,21 @@
             device_id_type=pl.DeviceIdType.MESH,
         ).wait_recv()
 
-    for peer in far + beside:
+    for peer in far[1::2] + [across, opposite] + far[0::2] + far_across[0::2] + [sibling]:
         send(me, peer)
-    for slot in far:
+    for slot in far[1::2]:
         arrive(slot)
         for peer in beside:
             send(slot, peer)
-    for first in beside:
-        for k in range(planes):
-            arrive(lax.rem(first + 4 * k, devices))
+    for slot in far[0::2] + far_across[0::2]:
+        arrive(slot)
+        send(slot, sibling)
+    for slot in [across, opposite] + far_across[1::2]:
+        arrive(slot)
+    for k in range(planes):
+        arrive(lax.rem(sibling + 4 * k, devices))
+    for k in range(1, planes):
+        arrive(lax.rem(opposite + 4 * k, devices))
     for copy in sent:
         copy.wait_send()
 
@@ -307,8 +318,7 @@
     request_ref,
     lookup_ref,
     content_ref,
-    switch_ref,
-    final_ref,
+    tail_ref,
     headterm_ref,
     update_ref,
     adjoint_ref,
@@ -374,8 +384,8 @@
     query = (product(x, request_ref[...]) * HEAD_DIMENSION ** (-0.5)).astype(jnp.bfloat16)
     keys = product(x, lookup_ref[...]).astype(jnp.bfloat16)
     values = product(x, content_ref[...]).astype(jnp.bfloat16)
-    gate = jax.nn.sigmoid(product(x, switch_ref[...]))
-    upstream = product(grad, final_ref[...], OUTER)
+    gate = jax.nn.sigmoid(product(x, tail_ref[0:channels, :]))
+    upstream = product(grad, tail_ref[channels:, :], OUTER)
     d_attn = (upstream * gate).astype(jnp.bfloat16)
 
     head_shape = (columns, span)
@@ -437,13 +447,13 @@
     pick_shape = (sequences, tokens)
     pick = one_where(iota(pick_shape, 1) == iota(pick_shape, 0) * residues + me)
     update_ref[...] = product(
-        product(pick, weighted).astype(jnp.bfloat16), final_ref[...]
+        product(pick, weighted).astype(jnp.bfloat16), tail_ref[channels:, :]
     ).astype(jnp.bfloat16)
 
     d_x = product(d_query, request_ref[...], OUTER)
     d_x = d_x + product(d_keys, lookup_ref[...], OUTER)
     d_x = d_x + product(d_values, content_ref[...], OUTER)
-    d_x = d_x + product(d_glog, switch_ref[...], OUTER)
+    d_x = d_x + product(d_glog, tail_ref[0:channels, :], OUTER)
     d_gain_ref[...] = jnp.sum(d_x * hat, axis=0, keepdims=True)
     d_msa = standardise_features_adjoint(d_x, hat, inv, gain).astype(jnp.bfloat16)
     adjoint_ref[...] = product(pick, d_msa).astype(jnp.bfloat16)
@@ -490,24 +500,18 @@
         alignment_existing_flags.T.astype(jnp.bfloat16),
         ((0, 0), (0, channels - pair_channels - sequences)),
     )
-    block = jnp.concatenate(
+    pair_block = jnp.concatenate(
         [
-            alignment_embedding.reshape(sequences, channels),
-            increment_adjoint.reshape(sequences, channels),
-            jnp.concatenate(
-                [
-                    couple_embedding.reshape(residues, pair_channels),
-                    jnp.broadcast_to(flags, (residues, channels - pair_channels)),
-                ],
-                axis=1,
-            ),
+            couple_embedding.reshape(residues, pair_channels),
+            jnp.broadcast_to(flags, (residues, channels - pair_channels)),
         ],
-        axis=0,
-    )
+        axis=1,
+    )
+    block_shape = (3 * sequences, channels)
     gathered = pl.pallas_call(
         lambda *refs: gather_kernel(devices, *refs),
-        out_shape=jax.ShapeDtypeStruct((devices, *block.shape), jnp.bfloat16),
-        in_specs=[vmem],
+        out_shape=jax.ShapeDtypeStruct((devices, *block_shape), jnp.bfloat16),
+        in_specs=[vmem] * 3,
         out_specs=vmem,
         scratch_shapes=[
             pltpu.SemaphoreType.DMA((devices - 1,)),
@@ -517,10 +521,14 @@
             collective_id=0, has_side_effects=True, vmem_limit_bytes=8 * 1024 * 1024
         ),
         cost_estimate=pl.CostEstimate(
-            flops=0, bytes_accessed=100 * devices * block.size * 2, transcendentals=0
+            flops=0, bytes_accessed=100 * devices * 3 * sequences * channels * 2, transcendentals=0
         ),
         name="gather_part",
-    )(block)
+    )(
+        alignment_embedding.reshape(sequences, channels),
+        increment_adjoint.reshape(sequences, channels),
+        pair_block,
+    )
     span = HEAD_NUMBER * HEAD_DIMENSION
     weight = jax.ShapeDtypeStruct((channels, span), jnp.float32)
     outs = pl.pallas_call(
@@ -538,7 +546,7 @@
             jax.ShapeDtypeStruct((1, channels), jnp.float32),
             jax.ShapeDtypeStruct((1, pair_channels), jnp.float32),
         ),
-        in_specs=[vmem] * 9,
+        in_specs=[vmem] * 8,
         out_specs=(vmem,) * 11,
         scratch_shapes=[pltpu.VMEM((residues, residues, pair_channels), jnp.bfloat16)],
         compiler_params=pltpu.CompilerParams(vmem_limit_bytes=24 * 1024 * 1024),
@@ -550,8 +558,7 @@
         request_matrix,
         lookup_matrix,
         content_matrix,
-        switch_matrix,
-        final_projection_matrix,
+        jnp.concatenate([switch_matrix, final_projection_matrix]),
         couple_to_headterm_matrix.T,
     )
     return (

time: 21.2 us -> 19.1 us (0.901)
  local copies, waits for them, and re-layouts: 2.53 us -> 0.73 us
  Pallas kernels: 16.9 us -> 16.4 us
  other arithmetic: 0.69 us -> 1.01 us
    unnamed x22 -> x20, local copies, waits for them, and re-layouts: 2.52 us -> 0.71 us
    pallas_call x1, Pallas kernels: 12.6 us -> 12.1 us  [on_device_whole_part(): pl.pallas_call(lambda *refs: gather_kernel(devices, *refs), out_shape=jax...]
    concatenate x1 -> x2, other arithmetic: 0.69 us -> 1 us  [the longest x1 1 us: on_device_whole_part(): jnp.concatenate([switch_matrix, final_projection_matrix])]
where the time goes in v4:
time: 19.1 us; the launch traced here: 18.9 us
  Pallas kernels  16.4 us (86%)
  other arithmetic  1.01 us (5%)
  between operations  0.8 us (4%)
  local copies, waits for them, and re-layouts  0.73 us (4%)
    pallas_call x1, Pallas kernels, on_device_whole_part(): pl.pallas_call(lambda *refs: gather_kernel(devices, *refs), out_shape=jax...  12.1 us
    pallas_call x1, Pallas kernels, on_device_whole_part(): pl.pallas_call(part_kernel, out_shape=(jax.ShapeDtypeStruct((sequences, c...  4.31 us
    concatenate x1, other arithmetic, on_device_whole_part(): jnp.concatenate([switch_matrix, final_projection_matrix])  1 us
    unnamed x20, local copies, waits for them, and re-layouts  0.71 us

profile of v4, /device:TPU:0, one launch (start us, length us, event | category | flops | bytes accessed | tf_op | source)
XLA Modules:
  0.0 18.9 jit_solution(10749365846184955886)
XLA Ops:
  0.6 0.0 copy-start.9
  0.7 0.0 copy-start.8
  0.7 0.6 %copy-done.9 = s32[16,1]{0,1:T(1,128)S(1)} copy-done((s32[16,1]{0,1:T(1,128)S(1)}, s32[16,1]{0,1:T(1,128)}, u32[]{:S(2)}) %copy-start.9) | copy-done | bytes 88
  1.3 0.0 copy-done.8
  1.4 0.0 copy-start.3
  1.4 0.0 copy-start.4
  1.4 1.0 %pad_maximum_fusion.tail_ref = bf16[512,256]{1,0:T(8,128)(2,1)S(1)} fusion(bf16[256,256]{1,0:T(8,128)(2,1)} %param.21, bf16[256,256]{1,0:T(8,128)(2,1)} %param.20), kind=kLoop, calls=%fused_computation | loop fusion | flops 524288 | bytes 524288 | tf_op jit(solution)/shard_map/concatenate | solution.py:561
  2.4 0.0 copy-done.3
  2.4 0.0 copy-done.4
  2.4 0.0 copy-start
  2.4 0.0 copy-start.1
  2.4 0.0 copy-start.2
  2.4 0.0 copy-start.5
  2.4 0.0 copy-start.6
  2.5 0.0 copy-start.7
  2.5 12.1 %gather_part.1.all_ref = bf16[16,48,256]{2,1,0:T(8,128)(2,1)S(1)} custom-call(bf16[16,256]{1,0:T(8,128)(2,1)S(1)} %bitcast.16, bf16[16,256]{1,0:T(8,128)(2,1)S(1)} %bitcast.17, bf16[16,256]{1,0:T(8,128)(2,1)S(1)} %pad_maximum_fusion.1.refs_2_), custom_call_target="tpu_custom_call" | custom-call | bytes 39321600 | tf_op jit(solution)/shard_map/gather_part/pallas_call | solution.py:511
  14.6 0.0 copy-done
  14.6 0.0 copy-done.1
  14.6 0.0 copy-done.2
  14.6 0.0 copy-done.5
  14.6 0.0 copy-done.6
  14.6 0.0 copy-done.7
  14.6 4.3 %whole_part.1 = (bf16[16,256]{1,0:T(8,128)(2,1)}, bf16[16,256]{1,0:T(8,128)(2,1)}, bf16[16,128]{1,0:T(8,128)(2,1)}, f32[256,256]{1,0:T(8,128)}, f32[256,256]{1,0...) custom-call(bf16[16,48,256]{2,1,0:T(8,128)(2,1)S(1)} %gather_part.1., ...), custom_call_target="tpu_custom_call" | custom-call | tf_op jit(solution)/shard_map/whole_part/pallas_call | solution.py:534
  (4 shorter events, 0.0 us)
Async XLA Ops:
  0.6 0.7 %copy-start.9 = (s32[16,1]{0,1:T(1,128)S(1)}, s32[16,1]{0,1:T(1,128)}, u32[]{:S(2)}) copy-start(s32[16,1]{0,1:T(1,128)} %param.13) | copy-start | bytes 196
  0.7 0.7 %copy-start.8 = (bf16[1,16,128]{2,1,0:T(8,128)(2,1)S(1)}, bf16[1,16,128]{2,1,0:T(8,128)(2,1)}, u32[]{:S(2)}) copy-start(bf16[1,16,128]{2,1,0:T(8,128)(2,1)} %param.14) | copy-start | bytes 12292
  1.4 1.0 %copy-start.3 = (bf16[16,1,256]{2,0,1:T(8,128)(2,1)S(1)}, bf16[16,1,256]{2,0,1:T(8,128)(2,1)}, u32[]{:S(2)}) copy-start(bf16[16,1,256]{2,0,1:T(8,128)(2,1)} %param.12) | copy-start | bytes 24580
  1.4 1.0 %copy-start.4 = (bf16[16,1,256]{2,0,1:T(8,128)(2,1)S(1)}, bf16[16,1,256]{2,0,1:T(8,128)(2,1)}, u32[]{:S(2)}) copy-start(bf16[16,1,256]{2,0,1:T(8,128)(2,1)} %param.23) | copy-start | bytes 24580
  2.4 12.2 %copy-start = (bf16[256,256]{1,0:T(8,128)(2,1)S(1)}, bf16[256,256]{1,0:T(8,128)(2,1)}, u32[]{:S(2)}) copy-start(bf16[256,256]{1,0:T(8,128)(2,1)} %request_ref.1) | copy-start | bytes 393220
  2.4 12.2 %copy-start.1 = (bf16[256,256]{1,0:T(8,128)(2,1)S(1)}, bf16[256,256]{1,0:T(8,128)(2,1)}, u32[]{:S(2)}) copy-start(bf16[256,256]{1,0:T(8,128)(2,1)} %lookup_ref.1) | copy-start | bytes 393220
  2.4 12.2 %copy-start.2 = (bf16[256,256]{1,0:T(8,128)(2,1)S(1)}, bf16[256,256]{1,0:T(8,128)(2,1)}, u32[]{:S(2)}) copy-start(bf16[256,256]{1,0:T(8,128)(2,1)} %content_ref.1) | copy-start | bytes 393220
  2.4 12.2 %copy-start.5 = (bf16[128,8]{0,1:T(8,128)(2,1)S(1)}, bf16[128,8]{0,1:T(8,128)(2,1)}, u32[]{:S(2)}) copy-start(bf16[128,8]{0,1:T(8,128)(2,1)} %param.22) | copy-start | bytes 6148
  2.4 12.2 %copy-start.6 = (f32[256]{0:T(256)S(1)}, f32[256]{0:T(256)}, u32[]{:S(2)}) copy-start(f32[256]{0:T(256)} %param.15) | copy-start | bytes 3076
  2.5 12.2 %copy-start.7 = (f32[128]{0:T(128)S(1)}, f32[128]{0:T(128)}, u32[]{:S(2)}) copy-start(f32[128]{0:T(128)} %param.16) | copy-start | bytes 1540

commit v5 on v4

--- a/solution.py
+++ b/solution.py
@@ -323,15 +323,21 @@
     update_ref,
     adjoint_ref,
     pair_adjoint_ref,
+    d_query_far,
+    d_key_far,
+    d_value_far,
+    d_gate_far,
+    d_out_far,
+    d_headterm_ref,
+    d_gain_ref,
+    d_pair_gain_ref,
+    pair_rows_ref,
     d_query_ref,
     d_key_ref,
     d_value_ref,
     d_gate_ref,
     d_out_ref,
-    d_headterm_ref,
-    d_gain_ref,
-    d_pair_gain_ref,
-    pair_rows_ref,
+    out_sem,
 ):
     me = lax.axis_index("dap")
     residues = all_ref.shape[0]
@@ -438,11 +444,18 @@
         axis=0,
     ).astype(jnp.bfloat16)
 
-    d_query_ref[...] = product(x, d_query, INNER)
-    d_key_ref[...] = product(x, d_keys, INNER)
-    d_value_ref[...] = product(x, d_values, INNER)
-    d_gate_ref[...] = product(x, d_glog, INNER)
-    d_out_ref[...] = product(weighted, grad, INNER)
+    leaving = []
+    for near, far, left, right in (
+        (d_out_ref, d_out_far, weighted, grad),
+        (d_gate_ref, d_gate_far, x, d_glog),
+        (d_query_ref, d_query_far, x, d_query),
+        (d_key_ref, d_key_far, x, d_keys),
+        (d_value_ref, d_value_far, x, d_values),
+    ):
+        near[...] = product(left, right, INNER)
+        copy = pltpu.make_async_copy(near, far, out_sem.at[len(leaving)])
+        copy.start()
+        leaving.append(copy)
 
     pick_shape = (sequences, tokens)
     pick = one_where(iota(pick_shape, 1) == iota(pick_shape, 0) * residues + me)
@@ -476,6 +489,8 @@
         .reshape(residues, residues, pair_lanes)
     )
     pair_adjoint_ref[...] = pair_rows_ref[me]
+    for copy in leaving:
+        copy.wait()
 
 
 def on_device_whole_part(
@@ -547,8 +562,13 @@
             jax.ShapeDtypeStruct((1, pair_channels), jnp.float32),
         ),
         in_specs=[vmem] * 8,
-        out_specs=(vmem,) * 11,
-        scratch_shapes=[pltpu.VMEM((residues, residues, pair_channels), jnp.bfloat16)],
+        out_specs=(vmem,) * 3 + (pl.BlockSpec(memory_space=pl.ANY),) * 5 + (vmem,) * 3,
+        scratch_shapes=[
+            pltpu.VMEM((residues, residues, pair_channels), jnp.bfloat16),
+            *[pltpu.VMEM((channels, span), jnp.float32)] * 4,
+            pltpu.VMEM((span, channels), jnp.float32),
+            pltpu.SemaphoreType.DMA((5,)),
+        ],
         compiler_params=pltpu.CompilerParams(vmem_limit_bytes=24 * 1024 * 1024),
         name="whole_part",
     )(

time: 19.1 us -> 19.9 us (1.042)
  Pallas kernels: 16.4 us -> 17.2 us
    pallas_call x1, Pallas kernels: 4.31 us -> 5.09 us  [on_device_whole_part(): pl.pallas_call(part_kernel, out_shape=(jax.ShapeDtypeStruct((sequences, c...]
where the time goes in v5:
time: 19.9 us; the launch traced here: 19.7 us
  Pallas kernels  17.2 us (86%)
  other arithmetic  1.01 us (5%)
  between operations  0.8 us (4%)
  local copies, waits for them, and re-layouts  0.73 us (4%)
    pallas_call x1, Pallas kernels, on_device_whole_part(): pl.pallas_call(lambda *refs: gather_kernel(devices, *refs), out_shape=jax...  12.1 us
    pallas_call x1, Pallas kernels, on_device_whole_part(): pl.pallas_call(part_kernel, out_shape=(jax.ShapeDtypeStruct((sequences, c...  5.09 us
    concatenate x1, other arithmetic, on_device_whole_part(): jnp.concatenate([switch_matrix, final_projection_matrix])  1 us
    unnamed x20, local copies, waits for them, and re-layouts  0.71 us

profile of v5, /device:TPU:0, one launch (start us, length us, event | category | flops | bytes accessed | tf_op | source)
XLA Modules:
  0.0 19.7 jit_solution(6082742984208439601)
XLA Ops:
  0.6 0.0 copy-start.9
  0.7 0.0 copy-start.8
  0.7 0.6 %copy-done.9 = s32[16,1]{0,1:T(1,128)S(1)} copy-done((s32[16,1]{0,1:T(1,128)S(1)}, s32[16,1]{0,1:T(1,128)}, u32[]{:S(2)}) %copy-start.9) | copy-done | bytes 88
  1.3 0.0 copy-done.8
  1.4 0.0 copy-start.3
  1.4 0.0 copy-start.4
  1.4 1.0 %pad_maximum_fusion.tail_ref = bf16[512,256]{1,0:T(8,128)(2,1)S(1)} fusion(bf16[256,256]{1,0:T(8,128)(2,1)} %param.21, bf16[256,256]{1,0:T(8,128)(2,1)} %param.20), kind=kLoop, calls=%fused_computation | loop fusion | flops 524288 | bytes 524288 | tf_op jit(solution)/shard_map/concatenate | solution.py:581
  2.4 0.0 copy-done.3
  2.4 0.0 copy-done.4
  2.4 0.0 copy-start
  2.4 0.0 copy-start.1
  2.4 0.0 copy-start.2
  2.4 0.0 copy-start.5
  2.4 0.0 copy-start.6
  2.5 0.0 copy-start.7
  2.5 12.1 %gather_part.1.all_ref = bf16[16,48,256]{2,1,0:T(8,128)(2,1)S(1)} custom-call(bf16[16,256]{1,0:T(8,128)(2,1)S(1)} %bitcast.16, bf16[16,256]{1,0:T(8,128)(2,1)S(1)} %bitcast.17, bf16[16,256]{1,0:T(8,128)(2,1)S(1)} %pad_maximum_fusion.1.refs_2_), custom_call_target="tpu_custom_call" | custom-call | bytes 39321600 | tf_op jit(solution)/shard_map/gather_part/pallas_call | solution.py:526
  14.6 0.0 copy-done
  14.6 0.0 copy-done.1
  14.6 0.0 copy-done.2
  14.6 0.0 copy-done.5
  14.6 0.0 copy-done.6
  14.6 0.0 copy-done.7
  14.6 5.1 %whole_part.1 = (bf16[16,256]{1,0:T(8,128)(2,1)}, bf16[16,256]{1,0:T(8,128)(2,1)}, bf16[16,128]{1,0:T(8,128)(2,1)}, f32[256,256]{1,0:T(8,128)}, f32[256,256]{1,0...) custom-call(bf16[16,48,256]{2,1,0:T(8,128)(2,1)S(1)} %gather_part.1., ...), custom_call_target="tpu_custom_call" | custom-call | tf_op jit(solution)/shard_map/whole_part/pallas_call | solution.py:549
  (4 shorter events, 0.0 us)
Async XLA Ops:
  0.6 0.7 %copy-start.9 = (s32[16,1]{0,1:T(1,128)S(1)}, s32[16,1]{0,1:T(1,128)}, u32[]{:S(2)}) copy-start(s32[16,1]{0,1:T(1,128)} %param.13) | copy-start | bytes 196
  0.7 0.7 %copy-start.8 = (bf16[1,16,128]{2,1,0:T(8,128)(2,1)S(1)}, bf16[1,16,128]{2,1,0:T(8,128)(2,1)}, u32[]{:S(2)}) copy-start(bf16[1,16,128]{2,1,0:T(8,128)(2,1)} %param.14) | copy-start | bytes 12292
  1.4 1.0 %copy-start.3 = (bf16[16,1,256]{2,0,1:T(8,128)(2,1)S(1)}, bf16[16,1,256]{2,0,1:T(8,128)(2,1)}, u32[]{:S(2)}) copy-start(bf16[16,1,256]{2,0,1:T(8,128)(2,1)} %param.12) | copy-start | bytes 24580
  1.4 1.0 %copy-start.4 = (bf16[16,1,256]{2,0,1:T(8,128)(2,1)S(1)}, bf16[16,1,256]{2,0,1:T(8,128)(2,1)}, u32[]{:S(2)}) copy-start(bf16[16,1,256]{2,0,1:T(8,128)(2,1)} %param.23) | copy-start | bytes 24580
  2.4 12.2 %copy-start = (bf16[256,256]{1,0:T(8,128)(2,1)S(1)}, bf16[256,256]{1,0:T(8,128)(2,1)}, u32[]{:S(2)}) copy-start(bf16[256,256]{1,0:T(8,128)(2,1)} %request_ref.1) | copy-start | bytes 393220
  2.4 12.2 %copy-start.1 = (bf16[256,256]{1,0:T(8,128)(2,1)S(1)}, bf16[256,256]{1,0:T(8,128)(2,1)}, u32[]{:S(2)}) copy-start(bf16[256,256]{1,0:T(8,128)(2,1)} %lookup_ref.1) | copy-start | bytes 393220
  2.4 12.2 %copy-start.2 = (bf16[256,256]{1,0:T(8,128)(2,1)S(1)}, bf16[256,256]{1,0:T(8,128)(2,1)}, u32[]{:S(2)}) copy-start(bf16[256,256]{1,0:T(8,128)(2,1)} %content_ref.1) | copy-start | bytes 393220
  2.4 12.2 %copy-start.5 = (bf16[128,8]{0,1:T(8,128)(2,1)S(1)}, bf16[128,8]{0,1:T(8,128)(2,1)}, u32[]{:S(2)}) copy-start(bf16[128,8]{0,1:T(8,128)(2,1)} %param.22) | copy-start | bytes 6148
  2.4 12.2 %copy-start.6 = (f32[256]{0:T(256)S(1)}, f32[256]{0:T(256)}, u32[]{:S(2)}) copy-start(f32[256]{0:T(256)} %param.15) | copy-start | bytes 3076
  2.5 12.2 %copy-start.7 = (f32[128]{0:T(128)S(1)}, f32[128]{0:T(128)}, u32[]{:S(2)}) copy-start(f32[128]{0:T(128)} %param.16) | copy-start | bytes 1540

commit v6 on v4

--- a/solution.py
+++ b/solution.py
@@ -252,8 +252,10 @@
             device_id_type=pl.DeviceIdType.MESH,
         ).wait_recv()
 
-    for peer in far[1::2] + [across, opposite] + far[0::2] + far_across[0::2] + [sibling]:
+    for peer in far[1::2] + [across] + far[0::2] + far_across[0::2] + [sibling]:
         send(me, peer)
+    arrive(across)
+    send(across, sibling)
     for slot in far[1::2]:
         arrive(slot)
         for peer in beside:
@@ -261,11 +263,10 @@
     for slot in far[0::2] + far_across[0::2]:
         arrive(slot)
         send(slot, sibling)
-    for slot in [across, opposite] + far_across[1::2]:
+    for slot in far_across[1::2]:
         arrive(slot)
     for k in range(planes):
         arrive(lax.rem(sibling + 4 * k, devices))
-    for k in range(1, planes):
         arrive(lax.rem(opposite + 4 * k, devices))
     for copy in sent:
         copy.wait_send()

time: 19.1 us -> 19.1 us (level)
  no operation moved by 1% of the time
where the time goes in v6:
time: 19.1 us; the launch traced here: 18.9 us
  Pallas kernels  16.4 us (86%)
  other arithmetic  1.01 us (5%)
  between operations  0.8 us (4%)
  local copies, waits for them, and re-layouts  0.73 us (4%)
    pallas_call x1, Pallas kernels, on_device_whole_part(): pl.pallas_call(lambda *refs: gather_kernel(devices, *refs), out_shape=jax...  12.1 us
    pallas_call x1, Pallas kernels, on_device_whole_part(): pl.pallas_call(part_kernel, out_shape=(jax.ShapeDtypeStruct((sequences, c...  4.31 us
    concatenate x1, other arithmetic, on_device_whole_part(): jnp.concatenate([switch_matrix, final_projection_matrix])  1 us
    unnamed x20, local copies, waits for them, and re-layouts  0.71 us

profile of v6, /device:TPU:0, one launch (start us, length us, event | category | flops | bytes accessed | tf_op | source)
XLA Modules:
  0.0 18.9 jit_solution(16863278044902878604)
XLA Ops:
  0.6 0.0 copy-start.9
  0.7 0.0 copy-start.8
  0.7 0.6 %copy-done.9 = s32[16,1]{0,1:T(1,128)S(1)} copy-done((s32[16,1]{0,1:T(1,128)S(1)}, s32[16,1]{0,1:T(1,128)}, u32[]{:S(2)}) %copy-start.9) | copy-done | bytes 88
  1.3 0.0 copy-done.8
  1.4 0.0 copy-start.3
  1.4 0.0 copy-start.4
  1.4 1.0 %pad_maximum_fusion.tail_ref = bf16[512,256]{1,0:T(8,128)(2,1)S(1)} fusion(bf16[256,256]{1,0:T(8,128)(2,1)} %param.21, bf16[256,256]{1,0:T(8,128)(2,1)} %param.20), kind=kLoop, calls=%fused_computation | loop fusion | flops 524288 | bytes 524288 | tf_op jit(solution)/shard_map/concatenate | solution.py:562
  2.4 0.0 copy-done.3
  2.4 0.0 copy-done.4
  2.4 0.0 copy-start
  2.4 0.0 copy-start.1
  2.4 0.0 copy-start.2
  2.4 0.0 copy-start.5
  2.4 0.0 copy-start.6
  2.5 0.0 copy-start.7
  2.5 12.1 %gather_part.1.all_ref = bf16[16,48,256]{2,1,0:T(8,128)(2,1)S(1)} custom-call(bf16[16,256]{1,0:T(8,128)(2,1)S(1)} %bitcast.16, bf16[16,256]{1,0:T(8,128)(2,1)S(1)} %bitcast.17, bf16[16,256]{1,0:T(8,128)(2,1)S(1)} %pad_maximum_fusion.1.refs_2_), custom_call_target="tpu_custom_call" | custom-call | bytes 39321600 | tf_op jit(solution)/shard_map/gather_part/pallas_call | solution.py:512
  14.6 0.0 copy-done
  14.6 0.0 copy-done.1
  14.6 0.0 copy-done.2
  14.6 0.0 copy-done.5
  14.6 0.0 copy-done.6
  14.6 0.0 copy-done.7
  14.6 4.3 %whole_part.1 = (bf16[16,256]{1,0:T(8,128)(2,1)}, bf16[16,256]{1,0:T(8,128)(2,1)}, bf16[16,128]{1,0:T(8,128)(2,1)}, f32[256,256]{1,0:T(8,128)}, f32[256,256]{1,0...) custom-call(bf16[16,48,256]{2,1,0:T(8,128)(2,1)S(1)} %gather_part.1., ...), custom_call_target="tpu_custom_call" | custom-call | tf_op jit(solution)/shard_map/whole_part/pallas_call | solution.py:535
  (4 shorter events, 0.0 us)
Async XLA Ops:
  0.6 0.7 %copy-start.9 = (s32[16,1]{0,1:T(1,128)S(1)}, s32[16,1]{0,1:T(1,128)}, u32[]{:S(2)}) copy-start(s32[16,1]{0,1:T(1,128)} %param.13) | copy-start | bytes 196
  0.7 0.7 %copy-start.8 = (bf16[1,16,128]{2,1,0:T(8,128)(2,1)S(1)}, bf16[1,16,128]{2,1,0:T(8,128)(2,1)}, u32[]{:S(2)}) copy-start(bf16[1,16,128]{2,1,0:T(8,128)(2,1)} %param.14) | copy-start | bytes 12292
  1.4 1.0 %copy-start.3 = (bf16[16,1,256]{2,0,1:T(8,128)(2,1)S(1)}, bf16[16,1,256]{2,0,1:T(8,128)(2,1)}, u32[]{:S(2)}) copy-start(bf16[16,1,256]{2,0,1:T(8,128)(2,1)} %param.12) | copy-start | bytes 24580
  1.4 1.0 %copy-start.4 = (bf16[16,1,256]{2,0,1:T(8,128)(2,1)S(1)}, bf16[16,1,256]{2,0,1:T(8,128)(2,1)}, u32[]{:S(2)}) copy-start(bf16[16,1,256]{2,0,1:T(8,128)(2,1)} %param.23) | copy-start | bytes 24580
  2.4 12.2 %copy-start = (bf16[256,256]{1,0:T(8,128)(2,1)S(1)}, bf16[256,256]{1,0:T(8,128)(2,1)}, u32[]{:S(2)}) copy-start(bf16[256,256]{1,0:T(8,128)(2,1)} %request_ref.1) | copy-start | bytes 393220
  2.4 12.2 %copy-start.1 = (bf16[256,256]{1,0:T(8,128)(2,1)S(1)}, bf16[256,256]{1,0:T(8,128)(2,1)}, u32[]{:S(2)}) copy-start(bf16[256,256]{1,0:T(8,128)(2,1)} %lookup_ref.1) | copy-start | bytes 393220
  2.4 12.2 %copy-start.2 = (bf16[256,256]{1,0:T(8,128)(2,1)S(1)}, bf16[256,256]{1,0:T(8,128)(2,1)}, u32[]{:S(2)}) copy-start(bf16[256,256]{1,0:T(8,128)(2,1)} %content_ref.1) | copy-start | bytes 393220
  2.4 12.2 %copy-start.5 = (bf16[128,8]{0,1:T(8,128)(2,1)S(1)}, bf16[128,8]{0,1:T(8,128)(2,1)}, u32[]{:S(2)}) copy-start(bf16[128,8]{0,1:T(8,128)(2,1)} %param.22) | copy-start | bytes 6148
  2.4 12.2 %copy-start.6 = (f32[256]{0:T(256)S(1)}, f32[256]{0:T(256)}, u32[]{:S(2)}) copy-start(f32[256]{0:T(256)} %param.15) | copy-start | bytes 3076
  2.5 12.2 %copy-start.7 = (f32[128]{0:T(128)S(1)}, f32[128]{0:T(128)}, u32[]{:S(2)}) copy-start(f32[128]{0:T(128)} %param.16) | copy-start | bytes 1540
